TPU v7x, 128 devices: a whole 4x4x4 slice. The times are simulated.
128 devices in a mesh: grp: 2 (over x_lo), px: 8 (over y, core), pz: 8 (over x_hi, z).
Axes of the slice: x: 4 (x_hi: 2, x_lo: 2; x = x_hi * 2 + x_lo), y: 4, z: 4, core: 2. Of those that a mesh axis runs over, the one named last changes fastest.
Arguments:
- cell_index: int32 [4096, 512], P(('px', 'pz')), may hold values from 0 to 255
- block_index: int32 [4096], P(('px', 'pz')), may hold values from 0 to 63
- volume: float32 [4096, 512], P(('px', 'pz')), may hold values from 0.2 to 2
- response_rate: float32 [4096, 512], P(('px', 'pz')), may hold values from 0.2 to 2
- spanwise_position: float32 [4096, 512], P(('px', 'pz')), may hold values from -3.140625 to 3.140625
- particle_velocity: float32 [3, 4096, 512], P(None, ('px', 'pz')), may hold values from -6 to 6
- seen_velocity: float32 [3, 4096, 512], P(None, ('px', 'pz')), may hold values from -6 to 6
- fluid_velocity: float32 [512, 3, 16, 2, 1024], P(None, None, ('grp', 'pz'), None, 'px'), may hold values from -6 to 6
- eigen_basis: float32 [512, 512], replicated, may hold values from -1 to 2, as said below
- eigen_inverse: float32 [512, 512], replicated, may hold values from -8 to 8, as said below
- eigenvalues: float32 [512], replicated, may hold values from 1 to 100000
Outputs:
- velocity_planes: bfloat16 [512, 3, 16, 2, 2048], P(('px', 'pz'), None, 'grp')
- updated_velocity: float32 [3, 4096, 512], P(None, ('px', 'pz'))
Inputs may be any that keep to these rules, and one draw needn't show every extreme that they name: eigen_inverse is the inverse of eigen_basis. eigen_basis has a dominant unit diagonal.
All inputs are finite; a program needn't handle non-finite values.
Results may differ from a plain program's by a relative error of at most 0.007.
Values may be sent and summed in bfloat16 or wider, within the bound.
A program may use at most 128 MiB of HBM per device.

v0:
```python
import math

import jax
import jax.numpy as jnp
from jax import lax
from jax.sharding import PartitionSpec as P

NX = 2048
KX = 1024
NY = 512
CB = 256
TILE_GROUP = 16


time_step = 0.5
gravity = 0.8
viscosity = 0.0001


def copy_for_each(x, axis):
    devices = lax.axis_size(axis)
    return lax.all_to_all(jnp.broadcast_to(x[None], (devices, *x.shape)), axis, 0, 0, tiled=True)


def over_copies(x, axis):
    return copy_for_each(x, axis).astype(jnp.float32).sum(axis=0)


def wave_table():
    positions = jnp.arange(NX, dtype=jnp.int32)
    stream_waves = jnp.arange(KX, dtype=jnp.int32) - KX // 2
    phase_turns = jnp.mod(positions[:, None] * stream_waves[None, :], NX)
    angles = phase_turns.astype(jnp.float32) * (2.0 * math.pi / NX)
    factor = 1.0 / math.sqrt(NX)
    return jnp.stack([jnp.cos(angles) * factor, jnp.sin(angles) * factor], axis=1).astype(
        jnp.bfloat16
    )


def on_device(
    cell_index,
    block_index,
    volume,
    response_rate,
    spanwise_position,
    particle_velocity,
    seen_velocity,
    fluid_velocity,
    eigen_basis,
    eigen_inverse,
    eigenvalues,
):
    highest = lax.Precision.HIGHEST
    group_index = lax.axis_index("grp")
    px_count = lax.axis_size("px")
    pz_count = lax.axis_size("pz")
    pencil_modes = fluid_velocity.shape[2]
    pencil_waves = fluid_velocity.shape[4]
    half_modes = pencil_modes * pz_count
    slab_rows = NY // (px_count * pz_count)
    strips = NX // CB
    tile_count = cell_index.shape[0]
    tile_size = cell_index.shape[1]
    rounds = tile_count // TILE_GROUP
    width_out = 8 * half_modes
    width_back = 6 * half_modes
    spanwise_waves = (group_index * half_modes + jnp.arange(half_modes) + 1).astype(jnp.float32)
    lanes = jnp.arange(CB, dtype=jnp.int32)
    forward_waves = wave_table()
    drag_force = volume * response_rate * (seen_velocity - particle_velocity)
    amounts = jnp.moveaxis(jnp.concatenate([volume[None], drag_force], axis=0), 0, -1)

    def deposit_turn(turn, totals):
        first_tile = turn * TILE_GROUP
        cell_slot = lax.dynamic_slice_in_dim(cell_index, first_tile, TILE_GROUP, 0)
        block_slot = lax.dynamic_slice_in_dim(block_index, first_tile, TILE_GROUP, 0)
        amount_slot = lax.dynamic_slice_in_dim(amounts, first_tile, TILE_GROUP, 0)
        angles = (
            lax.dynamic_slice_in_dim(spanwise_position, first_tile, TILE_GROUP, 0)[..., None]
            * spanwise_waves
        )
        phases = jnp.stack([jnp.cos(angles), -jnp.sin(angles)], axis=-2)
        payload = (amount_slot[..., :, None, None] * phases[..., None, :, :]).astype(jnp.bfloat16)
        payload = payload.reshape(TILE_GROUP, tile_size, width_out)
        one_hot = (cell_slot[..., None] == lanes).astype(jnp.bfloat16)
        shares = jnp.einsum("gpc,gpw->gwc", one_hot, payload, preferred_element_type=jnp.float32)
        return totals.at[block_slot].add(shares)

    totals = lax.fori_loop(
        0, rounds, deposit_turn, jnp.zeros((slab_rows * strips, width_out, CB), jnp.float32)
    )
    field = totals.astype(jnp.bfloat16).reshape(slab_rows, strips, width_out, CB)
    product = jnp.einsum(
        "ybwc,bcsi->ywsi",
        field,
        forward_waves.reshape(strips, CB, 2, KX),
        preferred_element_type=jnp.float32,
    )
    product = product.reshape(slab_rows, 4, 2, half_modes, 2, KX)
    real_part = product[:, :, 0, :, 0] + product[:, :, 1, :, 1]
    imag_part = product[:, :, 1, :, 0] - product[:, :, 0, :, 1]
    spectrum = jnp.stack([real_part, imag_part], axis=3).astype(jnp.bfloat16)
    outgoing = spectrum.reshape(slab_rows, 4, pz_count, pencil_modes, 2, px_count, pencil_waves)
    outgoing = jnp.transpose(outgoing, (5, 2, 0, 1, 3, 4, 6)).reshape(
        px_count * pz_count, slab_rows, 4, pencil_modes, 2, pencil_waves
    )
    pencil = lax.all_to_all(outgoing, ("px", "pz"), split_axis=0, concat_axis=0, tiled=True)
    pencil = pencil.reshape(NY, 4, pencil_modes, 2, pencil_waves)
    vertical = (jnp.arange(3) == 1).astype(jnp.float32)[None, :, None, None, None]
    force = pencil[:, 1:].astype(jnp.float32) - gravity * vertical * pencil[:, :1].astype(
        jnp.float32
    )
    stream_wave = (lax.axis_index("px") * pencil_waves + jnp.arange(pencil_waves) - KX // 2).astype(
        jnp.float32
    ) * 0.5
    span_wave = (
        group_index * half_modes
        + lax.axis_index("pz") * pencil_modes
        + jnp.arange(pencil_modes)
        + 1
    ).astype(jnp.float32)
    wave_square = (
        stream_wave[None, :] * stream_wave[None, :] + span_wave[:, None] * span_wave[:, None]
    )
    damping = 1.0 / (
        1.0
        + viscosity * (eigenvalues[:, None, None, None, None] + wave_square[None, None, :, None, :])
    )
    modal = jnp.einsum(
        "ij,jcmrk->icmrk", eigen_inverse, fluid_velocity + time_step * force, precision=highest
    )
    solved = jnp.einsum("ij,jcmrk->icmrk", eigen_basis, modal * damping, precision=highest).astype(
        jnp.bfloat16
    )
    inverse_waves = jnp.transpose(forward_waves, (2, 1, 0))
    returned = lax.all_to_all(
        solved.reshape(px_count * pz_count, slab_rows, 3, pencil_modes, 2, pencil_waves),
        ("px", "pz"),
        split_axis=0,
        concat_axis=0,
        tiled=True,
    )
    returned = returned.reshape(px_count, pz_count, slab_rows, 3, pencil_modes, 2, pencil_waves)
    product = jnp.einsum(
        "abycmrk,aksx->ycbmrsx",
        returned,
        inverse_waves.reshape(px_count, pencil_waves, 2, NX),
        preferred_element_type=jnp.float32,
    )
    product = product.reshape(slab_rows, 3, half_modes, 2, 2, NX)
    real_part = product[:, :, :, 0, 0] - product[:, :, :, 1, 1]
    imag_part = product[:, :, :, 0, 1] + product[:, :, :, 1, 0]
    velocity_planes = jnp.stack([real_part, imag_part], axis=3).astype(jnp.bfloat16)
    block_view = velocity_planes.reshape(slab_rows, width_back, strips, CB)

    def sample_turn(turn):
        first_tile = turn * TILE_GROUP
        cell_slot = lax.dynamic_slice_in_dim(cell_index, first_tile, TILE_GROUP, 0)
        block_slot = lax.dynamic_slice_in_dim(block_index, first_tile, TILE_GROUP, 0)
        angles = (
            lax.dynamic_slice_in_dim(spanwise_position, first_tile, TILE_GROUP, 0)[..., None]
            * spanwise_waves
        )
        block_rows = block_view[block_slot // strips, :, block_slot % strips, :]
        one_hot = (cell_slot[..., None] == lanes).astype(jnp.bfloat16)
        picked = jnp.einsum("gpc,gwc->gpw", one_hot, block_rows, preferred_element_type=jnp.float32)
        picked = picked.reshape(TILE_GROUP, tile_size, 3, half_modes, 2)
        return jnp.sum(
            picked[..., 0] * jnp.cos(angles)[:, :, None, :]
            - picked[..., 1] * jnp.sin(angles)[:, :, None, :],
            axis=-1,
        )

    sampled = lax.map(sample_turn, jnp.arange(rounds)).reshape(tile_count, tile_size, 3)
    mode_part = jnp.moveaxis(sampled, -1, 0)
    fluid_at = over_copies(mode_part.astype(jnp.bfloat16), "grp").astype(jnp.float32)
    upward = (jnp.arange(3) == 1).astype(jnp.float32)[:, None, None]
    updated_velocity = (
        particle_velocity
        + time_step * response_rate * (fluid_at - particle_velocity)
        - time_step * gravity * upward
    )
    return (velocity_planes, updated_velocity)


def solution(mesh):
    in_specs = (
        P(("px", "pz"), None),
        P(("px", "pz")),
        P(("px", "pz"), None),
        P(("px", "pz"), None),
        P(("px", "pz"), None),
        P(None, ("px", "pz"), None),
        P(None, ("px", "pz"), None),
        P(None, None, ("grp", "pz"), None, "px"),
        P(),
        P(),
        P(),
    )
    out_specs = (P(("px", "pz"), None, "grp", None, None), P(None, ("px", "pz"), None))
    return jax.shard_map(
        on_device, mesh=mesh, in_specs=in_specs, out_specs=out_specs, check_vma=False
    )
```

profile of v0, /device:TPU:1, one launch (start us, length us, event | category | flops | bytes accessed | tf_op | source)
XLA Modules:
  0.0 243.9 jit_solution(7122707955858757998)
XLA Ops:
  0.7 1.7 broadcast_multiply_fusion
  2.4 1.2 subtract_multiply_fusion
  4.6 2.5 %broadcast_in_dim.77 = f32[64,64,256]{2,1,0:T(8,128)} broadcast(f32[]{:T(128)} %constant.159.clone.1), dimensions={} | broadcast | bytes 4194308 | tf_op jit(solution)/shard_map/broadcast_in_dim | solution.py:90
  7.1 31.9 %while.27 = (s32[]{:T(128)}, f32[64,64,256]{2,1,0:T(8,128)}, s32[64]{0:T(128)S(1)}, f32[64,512,4]{1,0,2:T(8,128)S(1)}, f32[64,512]{1,0:T(8,128)S(1)}, /*index=5*...) while((s32[]{:T(128)}, f32[64,64,256]{2,1,0:T(8,128)}, ...), condition=%wide.region_2.3_spmd.clone, body=%wide.region_0.2_spmd.clone.sunk | while | flops 272105536 | bytes 9241007 | solution.py:89
  8.6 3.0 %fusion.67 = f32[16,64,256]{2,1,0:T(8,128)S(1)} fusion(bf16[16,512,64]{1,2,0:T(8,128)(2,1)S(1)} %bitcast.138, s32[16,512]{1,0:T(8,128)S(1)} %constant_dynamic-slice_fusion.12), kind=kOutput, calls=%fused_computation.7.clone.1 | convolution fusion | flops 270532608 | bytes 2129920 | tf_op jit(solution)/shard_map/while/body/eval_jaxpr/gpc,gpw->gwc/dot_general | solution.py:86
  11.7 3.4 %scatter_fusion = f32[64,64,256]{2,1,0:T(8,128)} fusion(f32[64,64,256]{2,1,0:T(8,128)} %get-tuple-element.516, s32[16]{0:T(128)S(1)} %compare_select_fusion.9, f32[16,64,256]{2,1,0:T(8,128)S(1)} %fusion.67), kind=kCustom, calls=%fused_computation.1.clone.clone.1 | custom fusion | flops 262144 | bytes 3145792 | tf_op jit(solution)/shard_map/while/body/eval_jaxpr/scatter-add | solution.py:87
  15.1 1.0 multiply_cosine_fusion.4
  16.5 3.0 %fusion.67 = f32[16,64,256]{2,1,0:T(8,128)S(1)} fusion(bf16[16,512,64]{1,2,0:T(8,128)(2,1)S(1)} %bitcast.138, s32[16,512]{1,0:T(8,128)S(1)} %constant_dynamic-slice_fusion.12), kind=kOutput, calls=%fused_computation.7.clone.1 | convolution fusion | flops 270532608 | bytes 2129920 | tf_op jit(solution)/shard_map/while/body/eval_jaxpr/gpc,gpw->gwc/dot_general | solution.py:86
  19.7 3.4 %scatter_fusion = f32[64,64,256]{2,1,0:T(8,128)} fusion(f32[64,64,256]{2,1,0:T(8,128)} %get-tuple-element.516, s32[16]{0:T(128)S(1)} %compare_select_fusion.9, f32[16,64,256]{2,1,0:T(8,128)S(1)} %fusion.67), kind=kCustom, calls=%fused_computation.1.clone.clone.1 | custom fusion | flops 262144 | bytes 3145792 | tf_op jit(solution)/shard_map/while/body/eval_jaxpr/scatter-add | solution.py:87
  24.5 3.0 %fusion.67 = f32[16,64,256]{2,1,0:T(8,128)S(1)} fusion(bf16[16,512,64]{1,2,0:T(8,128)(2,1)S(1)} %bitcast.138, s32[16,512]{1,0:T(8,128)S(1)} %constant_dynamic-slice_fusion.12), kind=kOutput, calls=%fused_computation.7.clone.1 | convolution fusion | flops 270532608 | bytes 2129920 | tf_op jit(solution)/shard_map/while/body/eval_jaxpr/gpc,gpw->gwc/dot_general | solution.py:86
  27.6 3.4 %scatter_fusion = f32[64,64,256]{2,1,0:T(8,128)} fusion(f32[64,64,256]{2,1,0:T(8,128)} %get-tuple-element.516, s32[16]{0:T(128)S(1)} %compare_select_fusion.9, f32[16,64,256]{2,1,0:T(8,128)S(1)} %fusion.67), kind=kCustom, calls=%fused_computation.1.clone.clone.1 | custom fusion | flops 262144 | bytes 3145792 | tf_op jit(solution)/shard_map/while/body/eval_jaxpr/scatter-add | solution.py:87
  32.5 3.0 %fusion.67 = f32[16,64,256]{2,1,0:T(8,128)S(1)} fusion(bf16[16,512,64]{1,2,0:T(8,128)(2,1)S(1)} %bitcast.138, s32[16,512]{1,0:T(8,128)S(1)} %constant_dynamic-slice_fusion.12), kind=kOutput, calls=%fused_computation.7.clone.1 | convolution fusion | flops 270532608 | bytes 2129920 | tf_op jit(solution)/shard_map/while/body/eval_jaxpr/gpc,gpw->gwc/dot_general | solution.py:86
  35.6 3.4 %scatter_fusion = f32[64,64,256]{2,1,0:T(8,128)} fusion(f32[64,64,256]{2,1,0:T(8,128)} %get-tuple-element.516, s32[16]{0:T(128)S(1)} %compare_select_fusion.9, f32[16,64,256]{2,1,0:T(8,128)S(1)} %fusion.67), kind=kCustom, calls=%fused_computation.1.clone.clone.1 | custom fusion | flops 262144 | bytes 3145792 | tf_op jit(solution)/shard_map/while/body/eval_jaxpr/scatter-add | solution.py:87
  39.0 2.5 %convert_element_type.107 = bf16[64,64,256]{2,1,0:T(8,128)(2,1)S(1)} convert(f32[64,64,256]{2,1,0:T(8,128)} %get-tuple-element.257) | non-fusion elementwise | flops 1048576 | bytes 6291456 | tf_op jit(solution)/shard_map/convert_element_type | solution.py:92
  41.5 35.2 %multiply_convert_fusion.2 = (bf16[8,256,1,1024]{3,1,0,2:T(8,128)(2,1)S(1)}, bf16[8,256,1,1024]{3,1,0,2:T(8,128)(2,1)S(1)}) fusion(s32[1024]{0:T(1024)S(1)} %iota_add_fusion, s32[8,256]{1,0:T(8,128)S(1)} %multiply_add_fusion), kind=kLoop, calls=%fused_computation.66 | loop fusion | flops 37748736 | bytes 8400896 | tf_op jit(solution)/shard_map/convert.5
  76.6 4.6 %fusion.34 = f32[8,4,2,8,2,1024]{5,3,4,2,1,0:T(8,128)S(1)} fusion(bf16[8,256,1,1024]{3,1,0,2:T(8,128)(2,1)S(1)} %get-tuple-element.397, bf16[8,256,1,1024]{3,1,0,2:T(8,128)(2,1)S(1)} %get-tuple-element.396, bf16[8,4,2,8,8,256,1]{5,3,2,1,4,0,6:T(8,128)(2,1)S(1)} %bitcast.146), kind=kOutput, calls=%fused_computation.74 | convolution fusion | flops 4311744512 | bytes 14680064 | tf_op jit(solution)/shard_map/ybwc,bcsi->ywsi/dot_general | solution.py:93
  81.9 2.1 copy.93
  83.9 12.4 %all-to-all-start = ((bf16[64,8,4,1,2,128]{5,4,2,1,3,0:T(2,128)(2,1)}), bf16[64,8,4,1,2,128]{5,4,2,1,3,0:T(2,128)(2,1)S(1)}, u32[]{:S(2)}, u32[]{:S(2)}) async-start(bf16[64,8,4,1,2,128]{5,4,2,1,3,0:T(2,128)(2,1)} %bitcast.17), calls=%async_computation | async-start | bytes 2097152 | tf_op jit(solution)/shard_map/all_to_all | solution.py:107
  96.5 19.2 %all-to-all-done = bf16[64,8,4,1,2,128]{5,4,2,1,3,0:T(2,128)(2,1)S(1)} async-done(((bf16[64,8,4,1,2,128]{5,4,2,1,3,0:T(2,128)(2,1)}), bf16[64,8,4,1,2,128]{5,4,2,1,3,0:T(2,128)(2,1)S(1)}, u32[]{:S(2)}, u32[]{:S(2)}) %all-to-all-start) | async-done | bytes 1048608 | tf_op jit(solution)/shard_map/all_to_all | solution.py:107
  115.9 2.8 %add_bitcast_fusion = f32[512,3,2,128]{3,2,1,0:T(2,128)S(1)} fusion(f32[512,3,1,2,128]{4,3,2,1,0:T(2,128)} %param.22, bf16[512,4,1,2,128]{4,3,2,1,0:T(2,128)(2,1)S(1)} %bitcast.144, f32[512,2,128]{2,1,0:T(2,128)S(1)} %fusion.53, f32[3]{0:T(128)S(1)} %compare_select_fusion.7), kind=kLoop, calls=%fused_computation.87 | loop fusion | flops 1966080 | bytes 4456460 | tf_op jit(solution)/shard_map/reshape.5
  118.8 5.1 %fusion.40 = f32[3,2,128,512]{3,2,1,0:T(8,128)S(1)} fusion(f32[512,3,2,128]{3,2,1,0:T(2,128)S(1)} %add_bitcast_fusion, f32[512,512]{1,0:T(8,128)S(1)} %copy-done), kind=kOutput, calls=%fused_computation.85 | convolution fusion | flops 2415919104 | bytes 4194304 | tf_op jit(solution)/shard_map/ij,jcmrk->icmrk/dot_general | solution.py:129
  123.9 2.7 %fusion.43 = bf16[512,3,2,128]{0,3,2,1:T(8,128)(2,1)S(1)} fusion(f32[3,2,128,512]{3,2,1,0:T(8,128)S(1)} %fusion.40, f32[512,512]{1,0:T(8,128)S(1)} %copy-done.4, f32[512,128]{0,1:T(8,128)S(1)} %add_divide_fusion), kind=kOutput, calls=%fused_computation.89 | convolution fusion | flops 2416705536 | bytes 3670016 | tf_op jit(solution)/shard_map/ij,jcmrk->icmrk/dot_general | solution.py:132
  126.9 1.0 copy.97
  128.0 4.5 %all-to-all-start.1 = ((bf16[64,8,3,1,2,128]{5,1,4,2,3,0:T(8,128)(2,1)}), bf16[64,8,3,1,2,128]{5,1,4,2,3,0:T(8,128)(2,1)S(1)}, u32[]{:S(2)}, u32[]{:S(2)}) async-start(bf16[64,8,3,1,2,128]{5,1,4,2,3,0:T(8,128)(2,1)} %copy.97), calls=%async_computation.1 | async-start | bytes 1572864 | tf_op jit(solution)/shard_map/all_to_all | solution.py:136
  132.5 37.2 %multiply_convert_fusion.4 = (bf16[2048,1,1024]{0,2,1:T(8,128)(2,1)}, bf16[2048,1,1024]{0,2,1:T(8,128)(2,1)}) fusion(s32[1024]{0:T(1024)S(1)} %iota_add_fusion), kind=kLoop, calls=%fused_computation.68 | loop fusion | flops 37748736 | bytes 8392704 | tf_op jit(solution)/shard_map/convert.7
  169.7 7.5 %pad_maximum_fusion.1 = bf16[2048,2,1024]{0,2,1:T(8,128)(2,1)} fusion(bf16[2048,1,1024]{0,2,1:T(8,128)(2,1)} %get-tuple-element.399, bf16[2048,1,1024]{0,2,1:T(8,128)(2,1)} %get-tuple-element.398), kind=kLoop, calls=%fused_computation.60 | loop fusion | flops 4194304 | bytes 16777216 | tf_op jit(solution)/shard_map/stack | solution.py:35
  177.1 5.9 %convolution_bitcast_fusion = f32[8,3,8,2,2,2048]{5,0,3,1,2,4:T(8,128)S(1)} fusion(bf16[8,128,2,2048,1,1,1]{3,1,0,6,5,4,2:T(8,128)(2,1)} %bitcast.139, bf16[8,8,8,3,2,128]{5,2,4,3,1,0:T(8,128)(2,1)S(1)} %bitcast.147), kind=kOutput, calls=%fused_computation.72 | convolution fusion | flops 3221225472 | bytes 15466496 | tf_op jit(solution)/shard_map/abycmrk,aksx->ycbmrsx/dot_general | solution.py:144
  184.3 2.0 copy.102
  186.3 46.4 %while.28 = (s32[]{:T(128)}, bf16[4,16,512,3]{2,1,0,3:T(8,128)(2,1)S(1)}, s32[4]{0:T(128)S(1)}, s32[64,512]{1,0:T(8,128)S(1)}, s32[64]{0:T(128)S(1)}, /*index=5*...) while((s32[]{:T(128)}, ...), condition=%wide.region_5.6_spmd.clone, body=%wide.region_3.5_spmd.clone.sunk | while | flops 204251648 | bytes 12026371 | solution.py:174
  187.7 2.0 gather_fusion
  189.8 3.2 %fusion.70 = f32[16,512,48]{1,2,0:T(8,128)} fusion(bf16[16,48,256]{2,1,0:T(8,128)(2,1)S(1)} %gather_fusion, s32[16,512]{1,0:T(8,128)S(1)} %constant_dynamic-slice_fusion.13), kind=kOutput, calls=%fused_computation.20.clone.1 | convolution fusion | flops 203423744 | bytes 1998848 | tf_op jit(solution)/shard_map/while/body/eval_jaxpr/gpc,gwc->gpw/dot_general | solution.py:166
  192.9 2.2 reshape.497
  195.2 1.2 fusion.71
  199.3 2.0 gather_fusion
  201.4 3.2 %fusion.70 = f32[16,512,48]{1,2,0:T(8,128)} fusion(bf16[16,48,256]{2,1,0:T(8,128)(2,1)S(1)} %gather_fusion, s32[16,512]{1,0:T(8,128)S(1)} %constant_dynamic-slice_fusion.13), kind=kOutput, calls=%fused_computation.20.clone.1 | convolution fusion | flops 203423744 | bytes 1998848 | tf_op jit(solution)/shard_map/while/body/eval_jaxpr/gpc,gwc->gpw/dot_general | solution.py:166
  204.5 2.2 reshape.497
  206.8 1.2 fusion.71
  210.9 2.0 gather_fusion
  213.0 3.2 %fusion.70 = f32[16,512,48]{1,2,0:T(8,128)} fusion(bf16[16,48,256]{2,1,0:T(8,128)(2,1)S(1)} %gather_fusion, s32[16,512]{1,0:T(8,128)S(1)} %constant_dynamic-slice_fusion.13), kind=kOutput, calls=%fused_computation.20.clone.1 | convolution fusion | flops 203423744 | bytes 1998848 | tf_op jit(solution)/shard_map/while/body/eval_jaxpr/gpc,gwc->gpw/dot_general | solution.py:166
  216.1 2.2 reshape.497
  218.4 1.2 fusion.71
  222.5 2.0 gather_fusion
  224.6 3.2 %fusion.70 = f32[16,512,48]{1,2,0:T(8,128)} fusion(bf16[16,48,256]{2,1,0:T(8,128)(2,1)S(1)} %gather_fusion, s32[16,512]{1,0:T(8,128)S(1)} %constant_dynamic-slice_fusion.13), kind=kOutput, calls=%fused_computation.20.clone.1 | convolution fusion | flops 203423744 | bytes 1998848 | tf_op jit(solution)/shard_map/while/body/eval_jaxpr/gpc,gwc->gpw/dot_general | solution.py:166
  227.7 2.2 reshape.497
  230.0 1.2 fusion.71
  233.5 3.5 %all-to-all-start.2 = ((bf16[2,3,64,512]{3,2,1,0:T(8,128)(2,1)}), bf16[2,3,64,512]{3,2,1,0:T(8,128)(2,1)S(1)}, u32[]{:S(2)}, u32[]{:S(2)}) async-start(bf16[2,3,64,512]{3,2,1,0:T(8,128)(2,1)} %broadcast_in_dim.80), calls=%async_computation.2 | async-start | bytes 786432 | tf_op jit(solution)/shard_map/all_to_all | solution.py:22
  237.0 4.2 %copy.104 = bf16[8,3,8,2,2048]{4,3,2,1,0:T(2,128)(2,1)} copy(bf16[8,3,8,2,2048]{4,0,1,2,3:T(8,128)(2,1)} %copy-done.2) | data formatting | bytes 3145728
  241.2 1.8 all-to-all-done.2
  (109 shorter events, 19.0 us)
Async XLA Ops:
  0.6 118.1 %copy-start = (f32[512,512]{1,0:T(8,128)S(1)}, f32[512,512]{1,0:T(8,128)}, u32[]{:S(2)}) copy-start(f32[512,512]{1,0:T(8,128)} %param.24) | copy-start | bytes 3145732
  0.6 6.4 %copy-start.6 = (s32[64,512]{1,0:T(8,128)S(1)}, s32[64,512]{1,0:T(8,128)}, u32[]{:S(2)}) copy-start(s32[64,512]{1,0:T(8,128)} %param.15) | copy-start | bytes 393220
  0.7 6.4 %copy-start.9 = (s32[64]{0:T(128)S(1)}, s32[64]{0:T(128)}, u32[]{:S(2)}) copy-start(s32[64]{0:T(128)} %param.16) | copy-start | bytes 772
  0.7 6.4 %copy-start.5 = (f32[64,512]{1,0:T(8,128)S(1)}, f32[64,512]{1,0:T(8,128)}, u32[]{:S(2)}) copy-start(f32[64,512]{1,0:T(8,128)} %param.19) | copy-start | bytes 393220
  81.7 14.6 %copy-start.8 = (f32[512]{0:T(512)S(1)}, f32[512]{0:T(512)}, u32[]{:S(2)}) copy-start(f32[512]{0:T(512)} %param.25) | copy-start | bytes 6148
  83.9 31.8 %all-to-all-start = ((bf16[64,8,4,1,2,128]{5,4,2,1,3,0:T(2,128)(2,1)}), bf16[64,8,4,1,2,128]{5,4,2,1,3,0:T(2,128)(2,1)S(1)}, u32[]{:S(2)}, u32[]{:S(2)}) async-start(bf16[64,8,4,1,2,128]{5,4,2,1,3,0:T(2,128)(2,1)} %bitcast.17), calls=%async_computation | async-start | bytes 2097152 | tf_op jit(solution)/shard_map/all_to_all | solution.py:107
  115.9 7.9 %copy-start.4 = (f32[512,512]{1,0:T(8,128)S(1)}, f32[512,512]{1,0:T(8,128)}, u32[]{:S(2)}) copy-start(f32[512,512]{1,0:T(8,128)} %param.23) | copy-start | bytes 3145732
  128.0 49.2 %all-to-all-start.1 = ((bf16[64,8,3,1,2,128]{5,1,4,2,3,0:T(8,128)(2,1)}), bf16[64,8,3,1,2,128]{5,1,4,2,3,0:T(8,128)(2,1)S(1)}, u32[]{:S(2)}, u32[]{:S(2)}) async-start(bf16[64,8,3,1,2,128]{5,1,4,2,3,0:T(8,128)(2,1)} %copy.97), calls=%async_computation.1 | async-start | bytes 1572864 | tf_op jit(solution)/shard_map/all_to_all | solution.py:136
  183.6 2.7 %copy-start.2 = (bf16[8,3,8,2,2048]{4,0,1,2,3:T(8,128)(2,1)}, bf16[8,3,8,2,2048]{4,0,1,2,3:T(8,128)(2,1)S(1)}, u32[]{:S(2)}) copy-start(bf16[8,3,8,2,2048]{4,0,1,2,3:T(8,128)(2,1)S(1)} %maximum_convert_fusion) | copy-start | bytes 4718596
  232.7 10.3 %copy-start.3 = (f32[3,64,512]{2,1,0:T(8,128)S(1)}, f32[3,64,512]{2,1,0:T(8,128)}, u32[]{:S(2)}) copy-start(f32[3,64,512]{2,1,0:T(8,128)} %param.20) | copy-start | bytes 1179652
  232.7 10.3 %copy-start.7 = (f32[64,512]{1,0:T(8,128)S(1)}, f32[64,512]{1,0:T(8,128)}, u32[]{:S(2)}) copy-start(f32[64,512]{1,0:T(8,128)} %get-tuple-element.394) | copy-start | bytes 393220
  232.7 11.2 %copy-start.1 = (f32[512,512]{1,0:T(8,128)S(1)}, f32[512,512]{1,0:T(8,128)}, u32[]{:S(2)}) copy-start(f32[512,512]{1,0:T(8,128)} %param.24) | copy-start | bytes 3145732
  233.5 9.4 %all-to-all-start.2 = ((bf16[2,3,64,512]{3,2,1,0:T(8,128)(2,1)}), bf16[2,3,64,512]{3,2,1,0:T(8,128)(2,1)S(1)}, u32[]{:S(2)}, u32[]{:S(2)}) async-start(bf16[2,3,64,512]{3,2,1,0:T(8,128)(2,1)} %broadcast_in_dim.80), calls=%async_computation.2 | async-start | bytes 786432 | tf_op jit(solution)/shard_map/all_to_all | solution.py:22
where the time goes:
time: 245 us; the launch traced here: 244 us
  other arithmetic  116 us (47%)
  matrix products  43.1 us (18%)
  local copies, waits for them, and re-layouts  38.7 us (16%)
  waiting for transfers between devices  21 us (9%)
  starting transfers between devices  20.4 us (8%)
  loops' own time  3.33 us (1%)
    another operation x3, other arithmetic  75.2 us
    all_to_all x1, waiting for transfers between devices, on_device(): lax.all_to_all(outgoing, ('px', 'pz'), split_axis=0, concat_axis=0, tiled...  19.2 us
    scatter-add x4, other arithmetic, deposit_turn(): return totals.at[block_slot].add(shares)  13.5 us
    dot_general x4, matrix products, sample_turn(): jnp.einsum('gpc,gwc->gpw', one_hot, block_rows, preferred_element_type=jn...  12.7 us
    all_to_all x1, starting transfers between devices, on_device(): lax.all_to_all(outgoing, ('px', 'pz'), split_axis=0, concat_axis=0, tiled...  12.4 us
    dot_general x4, matrix products, deposit_turn(): jnp.einsum('gpc,gpw->gwc', one_hot, payload, preferred_element_type=jnp.f...  12.2 us
    reshape x4, local copies, waits for them, and re-layouts, sample_turn(): picked = picked.reshape(TILE_GROUP, tile_size, 3, half_modes, 2)  8.88 us
    gather x4, local copies, waits for them, and re-layouts, sample_turn(): block_rows = block_view[block_slot // strips, :, block_slot % strips, :]  7.97 us
  transfers between devices with their start and end apart: 3, of which 2 were waited for; matrix products, arithmetic and copies ran while one was open for 20% of the time, Pallas kernels for 0%

commit v1 on v0

v1 whole, which is shorter than its diff:
```python
import math

import jax
import jax.numpy as jnp
import ml_dtypes
import numpy as np
from jax import lax
from jax.experimental import pallas as pl
from jax.experimental.pallas import tpu as pltpu
from jax.sharding import PartitionSpec as P

NX = 2048
KX = 1024
NY = 512
CB = 256
PT = 512
TILES = 64
MODES = 8
ROWS = 8
STRIPS = 8
WIDTH = 3 * 2 * MODES
BLOCKS = ROWS * STRIPS
FOLD = NX // 4
KEPT = KX // 4
N_PX = 8
N_PZ = 8
SLABS = N_PX * N_PZ
TURN = 1.0 / (2.0 * math.pi)
COSINE = (
    1.0,
    -19.73920440673828,
    64.93911743164062,
    -85.45011138916016,
    60.16743087768555,
    -25.96688461303711,
    6.527706146240234,
)

time_step = 0.5
gravity = 0.8
viscosity = 0.0001

f32 = jnp.float32
bf16 = jnp.bfloat16
VMEM = pl.BlockSpec(memory_space=pltpu.VMEM)
SMEM = pl.BlockSpec(memory_space=pltpu.SMEM)
ANY = pl.BlockSpec(memory_space=pl.ANY)


def wave_tables():
    x = np.arange(FOLD, dtype=np.int64)[None, :, None]
    k = (
        4 * np.arange(KEPT, dtype=np.int64)[None, None, :]
        + np.arange(4, dtype=np.int64)[:, None, None]
        - KX // 2
    )
    angle = np.mod(k * x, NX) * (2.0 * math.pi / NX)
    table = np.stack([np.cos(angle), np.sin(angle)], axis=1) / math.sqrt(NX)
    return table.astype(np.float32).astype(ml_dtypes.bfloat16)


def lane_order():
    perm = np.zeros((128, 128), np.float32)
    lanes = np.arange(128)
    perm[4 * (lanes % 32) + lanes // 32, lanes] = 1.0
    return np.concatenate([perm, perm], axis=0).astype(ml_dtypes.bfloat16)


def cosine_turns(turns):
    part = turns - jnp.round(turns)
    square = part * part
    value = jnp.full_like(square, COSINE[-1])
    for term in COSINE[-2::-1]:
        value = value * square + term
    return value


def one_hot_cells(cell_row):
    cells = jnp.broadcast_to(cell_row.astype(f32), (16, PT)).astype(bf16)
    lines = lax.broadcasted_iota(jnp.int32, (16, PT), 0).astype(f32).astype(bf16)
    one, zero = jnp.ones((16, PT), bf16), jnp.zeros((16, PT), bf16)
    return jnp.concatenate(
        [jnp.where(cells == lines + jnp.asarray(16 * i, bf16), one, zero) for i in range(16)],
        axis=0,
    )


def mode_turns(group):
    line = lax.broadcasted_iota(jnp.int32, (16, PT), 0)
    wave = (group * MODES + line // 2 + 1).astype(f32)
    shift = (line % 2).astype(f32) * 0.25
    return wave, shift


def swap_lanes(parts):
    return [
        jnp.concatenate([part[:, 32 * i : 32 * i + 32] for part in parts], axis=1)
        for i in range(4)
    ]


def dot(a, b):
    return lax.dot_general(a, b, (((1,), (0,)), ((), ())), preferred_element_type=f32)


def dot_t(a, b):
    return lax.dot_general(a, b, (((1,), (1,)), ((), ())), preferred_element_type=f32)


def deposit_kernel(block, cell, volume, rate, place, motion, seen, folded, totals):
    group = lax.axis_index("grp")
    wave, shift = mode_turns(group)
    totals[...] = jnp.zeros_like(totals)

    def eight_tiles(turn, carry):
        first = pl.multiple_of(turn * 8, 8)
        here = pl.ds(first, 8)
        cells = cell[here, :]
        amount = volume[here, :]
        scale = amount * rate[here, :]
        angle = place[here, :] * TURN
        drags = [scale * (seen[c, here, :] - motion[c, here, :]) for c in range(3)]
        drags[1] = drags[1] - gravity * amount
        for i in range(8):
            phase = cosine_turns(
                wave * jnp.broadcast_to(angle[i : i + 1, :], (16, PT)) + shift
            )
            payload = jnp.concatenate(
                [
                    (phase * jnp.broadcast_to(drags[c][i : i + 1, :], (16, PT))).astype(bf16)
                    for c in range(3)
                ],
                axis=0,
            )
            shares = dot_t(payload, one_hot_cells(cells[i : i + 1, :]))
            target = pl.ds(pl.multiple_of(block[first + i] * WIDTH, WIDTH), WIDTH)
            for h in range(2):
                totals[h, target, :] += shares[:, 128 * h : 128 * h + 128]
        return carry

    lax.fori_loop(0, TILES // 8, eight_tiles, 0)

    def fold(index, carry):
        c = index // MODES
        m = index % MODES
        for h in range(2):
            for s in range(2):
                field = [
                    [
                        totals[
                            h,
                            pl.ds(
                                (s + 2 * j) * WIDTH + c * 16 + m * 2 + z,
                                ROWS,
                                stride=STRIPS * WIDTH,
                            ),
                            :,
                        ]
                        for z in range(2)
                    ]
                    for j in range(4)
                ]
                re = [field[j][0] for j in range(4)]
                im = [field[j][1] for j in range(4)]
                sums = (re[0] + re[2], im[0] + im[2])
                others = (re[1] + re[3], im[1] + im[3])
                lefts = (re[0] - re[2], im[0] - im[2])
                rights = (re[1] - re[3], im[1] - im[3])
                results = (
                    (sums[0] + others[0], sums[1] + others[1]),
                    (lefts[0] + rights[1], lefts[1] - rights[0]),
                    (sums[0] - others[0], sums[1] - others[1]),
                    (lefts[0] - rights[1], lefts[1] + rights[0]),
                )
                for q in range(4):
                    pair = jnp.concatenate(results[q], axis=0)
                    lanes = slice(s * 256 + h * 128, s * 256 + h * 128 + 128)
                    folded[q, c, m, :, lanes] = pair.astype(bf16)
        return carry

    lax.fori_loop(0, 3 * MODES, fold, 0)


def flow_kernel(
    folded,
    block,
    cell,
    rate,
    place,
    motion,
    tables,
    order,
    fluid_any,
    basis_any,
    inverse_any,
    eigenvalues,
    planes_out,
    updated,
    fluid,
    basis,
    inverse,
    split_basis,
    split_inverse,
    damping,
    ordered,
    forward_send,
    forward_recv,
    back_send,
    back_recv,
    planes,
    blocks,
    part,
    part_send,
    part_recv,
    load_sem,
    own_sem,
    send_sem,
    recv_sem,
    part_send_sem,
    part_recv_sem,
):
    grp = lax.axis_index("grp")
    px = lax.axis_index("px")
    pz = lax.axis_index("pz")
    me = px * N_PZ + pz

    def peer(step):
        return lax.rem(px + step // N_PZ, N_PX), lax.rem(pz + lax.rem(step, N_PZ), N_PZ)

    barrier = pltpu.get_barrier_semaphore()

    def greet(step, carry):
        a, b = peer(step)
        pl.semaphore_signal(barrier, inc=1, device_id={"px": a, "pz": b})
        return carry

    loads = [
        pltpu.make_async_copy(fluid_any, fluid, load_sem.at[0]),
        pltpu.make_async_copy(basis_any, basis, load_sem.at[1]),
        pltpu.make_async_copy(inverse_any, inverse, load_sem.at[2]),
    ]
    for load in loads:
        load.start()
    pl.semaphore_signal(barrier, inc=1, device_id={"grp": 1 - grp})
    lax.fori_loop(1, SLABS, greet, 0)

    def forward(c):
        classes = []
        for q in range(4):
            rows = folded[q, c].reshape(MODES * 16, FOLD)
            even = dot(rows, tables[q, 0]).reshape(MODES, 2, ROWS, KEPT)
            odd = dot(rows, tables[q, 1]).reshape(MODES, 2, ROWS, KEPT)
            re = even[:, 0] + odd[:, 1]
            im = even[:, 1] - odd[:, 0]
            classes.append(
                jnp.concatenate([re, im], axis=1).reshape(MODES * 16, KEPT)
            )
        for h in range(2):
            chunks = swap_lanes([item[:, 128 * h : 128 * h + 128] for item in classes])
            for i in range(4):
                first = (4 * h + i) * 128
                forward_send[c, :, :, first : first + 128] = (
                    chunks[i].astype(bf16).reshape(MODES, 16, 128)
                )

    def forward_start(c):
        def send(step, carry):
            a, b = peer(step)
            pltpu.make_async_remote_copy(
                forward_send.at[c, b, :, pl.ds(pl.multiple_of(a * 128, 128), 128)],
                forward_recv.at[c, me],
                send_sem.at[c],
                recv_sem.at[c],
                device_id={"px": a, "pz": b},
            ).start()
            return carry

        pltpu.make_async_copy(
            forward_send.at[c, pz, :, pl.ds(pl.multiple_of(px * 128, 128), 128)],
            forward_recv.at[c, me],
            own_sem.at[c],
        ).start()
        lax.fori_loop(1, SLABS, send, 0)

    def back_start(c):
        def send(step, carry):
            a, b = peer(step)
            pltpu.make_async_remote_copy(
                back_send.at[c, a * N_PZ + b],
                back_recv.at[c, pz, :, pl.ds(pl.multiple_of(px * 128, 128), 128)],
                send_sem.at[3 + c],
                recv_sem.at[3 + c],
                device_id={"px": a, "pz": b},
            ).start()
            return carry

        pltpu.make_async_copy(
            back_send.at[c, me],
            back_recv.at[c, pz, :, pl.ds(pl.multiple_of(px * 128, 128), 128)],
            own_sem.at[3 + c],
        ).start()
        lax.fori_loop(1, SLABS, send, 0)

    def exchange_wait(index):
        blocks = forward_recv.at[0, pl.ds(0, SLABS - 1)]
        pltpu.make_async_remote_copy(
            blocks,
            blocks,
            send_sem.at[index],
            recv_sem.at[index],
            device_id={"px": px, "pz": pz},
        ).wait_recv()
        own = forward_recv.at[0, 0]
        pltpu.make_async_copy(own, own, own_sem.at[index]).wait()

    def sent_wait(index):
        blocks = forward_recv.at[0, pl.ds(0, SLABS - 1)]
        pltpu.make_async_remote_copy(
            blocks,
            blocks,
            send_sem.at[index],
            recv_sem.at[index],
            device_id={"px": px, "pz": pz},
        ).wait_send()

    forward(0)
    pl.semaphore_wait(barrier, SLABS)
    forward_start(0)
    forward(1)
    forward_start(1)
    forward(2)
    forward_start(2)

    for load in loads:
        load.wait()
    for matrix, split in ((basis, split_basis), (inverse, split_inverse)):
        high = matrix[...].astype(bf16)
        split[0] = high
        split[1] = (matrix[...] - high.astype(f32)).astype(bf16)
    lane = lax.broadcasted_iota(jnp.int32, (1, 128), 1)
    wave = px * 128 + 4 * (lane % 32) + lane // 32 - KX // 2
    wave = wave.astype(f32) * 0.5
    span = (grp * MODES + pz + 1).astype(f32)
    square = wave * wave + span * span
    column = jnp.transpose(jnp.broadcast_to(eigenvalues[...], (128, NY)))
    damping[...] = 1.0 / (1.0 + viscosity * (column + square))
    for c in range(3):
        for r in range(2):
            state = fluid[pl.ds(c * 2 + r, NY, stride=6), :]
            high = state.astype(bf16)
            low = (state - high.astype(f32)).astype(bf16)
            ordered[c, :, 128 * r : 128 * r + 128] = dot(
                jnp.concatenate([high, low], axis=1), order[...]
            )

    def apply(split, value):
        high = value.astype(bf16)
        low = (value - high.astype(f32)).astype(bf16)
        return dot(split[0], high) + (dot(split[0], low) + dot(split[1], high))

    for c in range(3):
        exchange_wait(c)
        forcing = forward_recv[c].astype(f32)
        force = jnp.concatenate(
            [forcing[:, 8 * r : 8 * r + 8, :].reshape(NY, 128) for r in range(2)], axis=1
        )
        modal = apply(split_inverse, ordered[c] + time_step * force)
        damp = damping[...]
        solved = apply(split_basis, modal * jnp.concatenate([damp, damp], axis=1))
        back_send[c] = jnp.concatenate(
            [solved[:, 128 * r : 128 * r + 128].reshape(SLABS, ROWS, 128) for r in range(2)],
            axis=1,
        ).astype(bf16)
        back_start(c)

    def backward(c):
        halves = []
        for h in range(2):
            parts = [
                back_recv[c, :, :, (4 * h + i) * 128 : (4 * h + i) * 128 + 128].reshape(
                    MODES * 16, 128
                )
                for i in range(4)
            ]
            halves.append(swap_lanes(parts))
        re, im = [], []
        for q in range(4):
            rows = jnp.concatenate([halves[0][q], halves[1][q]], axis=1)
            even = dot_t(rows, tables[q, 0]).reshape(MODES, 2, ROWS, FOLD)
            odd = dot_t(rows, tables[q, 1]).reshape(MODES, 2, ROWS, FOLD)
            re.append(even[:, 0] - odd[:, 1])
            im.append(odd[:, 0] + even[:, 1])
        sums = (re[0] + re[2], im[0] + im[2])
        lefts = (re[0] - re[2], im[0] - im[2])
        others = (re[1] + re[3], im[1] + im[3])
        rights = (im[3] - im[1], re[1] - re[3])
        results = (
            (sums[0] + others[0], sums[1] + others[1]),
            (lefts[0] + rights[0], lefts[1] + rights[1]),
            (sums[0] - others[0], sums[1] - others[1]),
            (lefts[0] - rights[0], lefts[1] - rights[1]),
        )
        for j in range(4):
            for r in range(2):
                for m in range(MODES):
                    for s in range(2):
                        for h in range(2):
                            lanes = slice(s * 256 + h * 128, s * 256 + h * 128 + 128)
                            planes[
                                h,
                                pl.ds(
                                    (2 * j + s) * WIDTH + c * 16 + m * 2 + r,
                                    ROWS,
                                    stride=STRIPS * WIDTH,
                                ),
                                :,
                            ] = results[j][r][m, :, lanes]

    for c in range(3):
        exchange_wait(3 + c)
        backward(c)

    def write_row(y, carry):
        for s in range(STRIPS):
            source = pl.ds(pl.multiple_of((y * STRIPS + s) * WIDTH, WIDTH), WIDTH)
            for h in range(2):
                value = planes[h, source, :].astype(bf16)
                lanes = slice(s * 256 + h * 128, s * 256 + h * 128 + 128)
                planes_out[y, :, lanes] = value
                blocks[y * STRIPS + s, :, 128 * h : 128 * h + 128] = value
        return carry

    lax.fori_loop(0, ROWS, write_row, 0)

    wave, shift = mode_turns(grp)

    def part_copy(turn):
        here = pl.ds(pl.multiple_of(turn * 16, 16), 16)
        return pltpu.make_async_remote_copy(
            part_send.at[:, here, :],
            part_recv.at[:, here, :],
            part_send_sem.at[turn],
            part_recv_sem.at[turn],
            device_id={"grp": 1 - grp},
        )

    def sixteen_tiles(turn, carry):
        for half in range(2):
            first = pl.multiple_of(turn * 16 + 8 * half, 8)
            here = pl.ds(first, 8)
            cells = cell[here, :]
            angle = place[here, :] * TURN
            lines = [[], [], []]
            for i in range(8):
                phase = cosine_turns(
                    wave * jnp.broadcast_to(angle[i : i + 1, :], (16, PT)) + shift
                )
                picked = dot(blocks[block[first + i]], one_hot_cells(cells[i : i + 1, :]))
                for c in range(3):
                    lines[c].append(
                        jnp.sum(picked[16 * c : 16 * c + 16, :] * phase, axis=0, keepdims=True)
                    )
            for c in range(3):
                part[c, here, :] = jnp.concatenate(lines[c], axis=0)
        here = pl.ds(pl.multiple_of(turn * 16, 16), 16)
        for c in range(3):
            part_send[c, here, :] = part[c, here, :].astype(bf16)
        part_copy(turn).start()
        return carry

    lax.fori_loop(0, TILES // 16, sixteen_tiles, 0)

    def update(turn, carry):
        part_copy(turn).wait()
        here = pl.ds(pl.multiple_of(turn * 16, 16), 16)
        for c in range(3):
            fluid_at = part_send[c, here, :].astype(f32) + part_recv[c, here, :].astype(f32)
            old = motion[c, here, :]
            new = old + time_step * rate[here, :] * (fluid_at - old)
            updated[c, here, :] = new - time_step * gravity if c == 1 else new
        return carry

    lax.fori_loop(0, TILES // 16, update, 0)
    for index in range(6):
        sent_wait(index)


def on_device(
    cell_index,
    block_index,
    volume,
    response_rate,
    spanwise_position,
    particle_velocity,
    seen_velocity,
    fluid_velocity,
    eigen_basis,
    eigen_inverse,
    eigenvalues,
):
    folded = pl.pallas_call(
        deposit_kernel,
        out_shape=jax.ShapeDtypeStruct((4, 3, MODES, 16, FOLD), bf16),
        in_specs=[SMEM] + [VMEM] * 6,
        out_specs=VMEM,
        scratch_shapes=[pltpu.VMEM((2, BLOCKS * WIDTH, 128), f32)],
        compiler_params=pltpu.CompilerParams(vmem_limit_bytes=40 * 2**20),
        name="deposit",
    )(
        block_index,
        cell_index,
        volume,
        response_rate,
        spanwise_position,
        particle_velocity,
        seen_velocity,
    )
    tables = jnp.asarray(wave_tables())
    order = jnp.asarray(lane_order())
    planes, updated = pl.pallas_call(
        flow_kernel,
        out_shape=(
            jax.ShapeDtypeStruct((ROWS, WIDTH, NX), bf16),
            jax.ShapeDtypeStruct((3, TILES, PT), f32),
        ),
        in_specs=[VMEM, SMEM] + [VMEM] * 6 + [ANY] * 3 + [VMEM],
        out_specs=(VMEM, VMEM),
        scratch_shapes=[
            pltpu.VMEM((NY * 6, 128), f32),
            pltpu.VMEM((NY, NY), f32),
            pltpu.VMEM((NY, NY), f32),
            pltpu.VMEM((2, NY, NY), bf16),
            pltpu.VMEM((2, NY, NY), bf16),
            pltpu.VMEM((NY, 128), f32),
            pltpu.VMEM((3, NY, 256), f32),
            pltpu.VMEM((3, MODES, 16, KX), bf16),
            pltpu.VMEM((3, SLABS, 16, 128), bf16),
            pltpu.VMEM((3, SLABS, 16, 128), bf16),
            pltpu.VMEM((3, MODES, 16, KX), bf16),
            pltpu.VMEM((2, BLOCKS * WIDTH, 128), f32),
            pltpu.VMEM((BLOCKS, WIDTH, CB), bf16),
            pltpu.VMEM((3, TILES, PT), f32),
            pltpu.VMEM((3, TILES, PT), bf16),
            pltpu.VMEM((3, TILES, PT), bf16),
            pltpu.SemaphoreType.DMA((3,)),
            pltpu.SemaphoreType.DMA((6,)),
            pltpu.SemaphoreType.DMA((6,)),
            pltpu.SemaphoreType.DMA((6,)),
            pltpu.SemaphoreType.DMA((TILES // 16,)),
            pltpu.SemaphoreType.DMA((TILES // 16,)),
        ],
        compiler_params=pltpu.CompilerParams(
            collective_id=0, has_side_effects=True, vmem_limit_bytes=56 * 2**20
        ),
        name="flow",
    )(
        folded,
        block_index,
        cell_index,
        response_rate,
        spanwise_position,
        particle_velocity,
        tables,
        order,
        fluid_velocity.reshape(NY * 6, 128),
        eigen_basis,
        eigen_inverse,
        eigenvalues.reshape(1, NY),
    )
    return planes.reshape(ROWS, 3, MODES, 2, NX), updated


def solution(mesh):
    in_specs = (
        P(("px", "pz"), None),
        P(("px", "pz")),
        P(("px", "pz"), None),
        P(("px", "pz"), None),
        P(("px", "pz"), None),
        P(None, ("px", "pz"), None),
        P(None, ("px", "pz"), None),
        P(None, None, ("grp", "pz"), None, "px"),
        P(),
        P(),
        P(),
    )
    out_specs = (P(("px", "pz"), None, "grp", None, None), P(None, ("px", "pz"), None))
    return jax.shard_map(
        on_device, mesh=mesh, in_specs=in_specs, out_specs=out_specs, check_vma=False
    )
```

time: 245 us -> 67.7 us (0.28)
  other arithmetic: 116 us -> 0 us
  Pallas kernels: 0 us -> 54.7 us
  matrix products: 43.1 us -> 0 us
  local copies, waits for them, and re-layouts: 38.7 us -> 11.9 us
  waiting for transfers between devices: 21 us -> 0 us
  starting transfers between devices: 20.4 us -> 0 us
  loops' own time: 3.33 us -> 0 us
    another operation x9 -> x0, other arithmetic: 83.3 us -> none
    pallas_call x0 -> x2, Pallas kernels: none -> 54.7 us  [the longest x1 45.7 us: on_device(): pl.pallas_call(flow_kernel, out_shape=(jax.ShapeDtypeStruct((ROWS, WIDTH,...]
    dot_general x12 -> x0, matrix products: 43.1 us -> none  [the longest x4 12.7 us: sample_turn(): jnp.einsum('gpc,gwc->gpw', one_hot, block_rows, preferred_element_type=jn...]
    all_to_all x3 -> x0, waiting for transfers between devices: 21 us -> none  [the longest x1 19.2 us: on_device(): lax.all_to_all(outgoing, ('px', 'pz'), split_axis=0, concat_axis=0, tiled...]
    all_to_all x3 -> x0, starting transfers between devices: 20.4 us -> none  [the longest x1 12.4 us: on_device(): lax.all_to_all(outgoing, ('px', 'pz'), split_axis=0, concat_axis=0, tiled...]
    scatter-add x4 -> x0, other arithmetic: 13.5 us -> none  [deposit_turn(): return totals.at[block_slot].add(shares)]
    gather x4 -> x0, local copies, waits for them, and re-layouts: 7.97 us -> none  [sample_turn(): block_rows = block_view[block_slot // strips, :, block_slot % strips, :]]
    cos x8 -> x0, other arithmetic: 7.92 us -> none  [the longest x4 3.98 us: deposit_turn(): phases = jnp.stack([jnp.cos(angles), -jnp.sin(angles)], axis=-2)]
  transfers between devices with their start and end apart: 3 -> 0, of which waited for: 2 -> 0; matrix products, arithmetic and copies ran while one was open for 20% -> 0% of each run, Pallas kernels for 0% -> 0%
where the time goes in v1:
time: 67.7 us; the launch traced here: 67.3 us
  Pallas kernels  54.7 us (81%)
  local copies, waits for them, and re-layouts  11.9 us (18%)
  between operations  0.68 us (1%)
    pallas_call x1, Pallas kernels, on_device(): pl.pallas_call(flow_kernel, out_shape=(jax.ShapeDtypeStruct((ROWS, WIDTH,...  45.7 us
    pallas_call x1, Pallas kernels, on_device(): pl.pallas_call(deposit_kernel, out_shape=jax.ShapeDtypeStruct((4, 3, MODE...  9.02 us
    unnamed x19, local copies, waits for them, and re-layouts  8.14 us
    reshape x1, local copies, waits for them, and re-layouts, on_device(): return (planes.reshape(ROWS, 3, MODES, 2, NX), updated)  3.8 us

profile of v1, /device:TPU:1, one launch (start us, length us, event | category | flops | bytes accessed | tf_op | source)
XLA Modules:
  0.0 67.3 jit_solution(16373478418912469394)
XLA Ops:
  0.6 0.0 copy-start.1
  0.6 1.0 %copy-done.1 = f32[3,64,512]{2,1,0:T(8,128)S(1)} copy-done((f32[3,64,512]{2,1,0:T(8,128)S(1)}, f32[3,64,512]{2,1,0:T(8,128)}, u32[]{:S(2)}) %copy-start.1) | copy-done | bytes 393240
  1.6 0.0 copy-start.2
  1.6 0.9 %copy-done.2 = s32[64,512]{1,0:T(8,128)S(1)} copy-done((s32[64,512]{1,0:T(8,128)S(1)}, s32[64,512]{1,0:T(8,128)}, u32[]{:S(2)}) %copy-start.2) | copy-done | bytes 131096
  2.5 0.0 copy-start.3
  2.5 0.9 %copy-done.3 = f32[64,512]{1,0:T(8,128)S(1)} copy-done((f32[64,512]{1,0:T(8,128)S(1)}, f32[64,512]{1,0:T(8,128)}, u32[]{:S(2)}) %copy-start.3) | copy-done | bytes 131096
  3.4 0.0 copy-start.4
  3.4 0.9 %copy-done.4 = f32[64,512]{1,0:T(8,128)S(1)} copy-done((f32[64,512]{1,0:T(8,128)S(1)}, f32[64,512]{1,0:T(8,128)}, u32[]{:S(2)}) %copy-start.4) | copy-done | bytes 131096
  4.3 0.0 copy-start.5
  4.3 1.0 %copy-done.5 = f32[3,64,512]{2,1,0:T(8,128)S(1)} copy-done((f32[3,64,512]{2,1,0:T(8,128)S(1)}, f32[3,64,512]{2,1,0:T(8,128)}, u32[]{:S(2)}) %copy-start.5) | copy-done | bytes 393240
  5.3 0.0 copy-start.6
  5.3 0.9 %copy-done.6 = f32[64,512]{1,0:T(8,128)S(1)} copy-done((f32[64,512]{1,0:T(8,128)S(1)}, f32[64,512]{1,0:T(8,128)}, u32[]{:S(2)}) %copy-start.6) | copy-done | bytes 131096
  6.2 0.0 copy-start.7
  6.2 0.7 copy-done.7
  6.9 9.0 %deposit.1.folded = bf16[4,3,8,16,512]{4,3,2,1,0:T(8,128)(2,1)S(1)} custom-call(s32[64]{0:T(128)S(1)} %copy-done.7, s32[64,512]{1,0:T(8,128)S(1)} %copy-done.2, f32[64,512]{1,0:T(8,128)S(1)} %copy-done.6, f32[64,512]{1,0:T(8,128)S(1)} %copy-done.3, f32[64,512]{1,0:T(8,128)S(1)} %copy-done.4, f32[3,64,512]{2,1,0:T(8,128)S(1)} %copy-done.1, ...), custom_call_target="tpu_custom_call" | custom-call | tf_op jit(solution)/shard_map/deposit/pallas_call | solution.py:501
  15.9 0.0 copy-start
  15.9 1.1 %copy-done = bf16[4,3,8,16,512]{4,3,2,1,0:T(8,128)(2,1)} copy-done((bf16[4,3,8,16,512]{4,3,2,1,0:T(8,128)(2,1)}, bf16[4,3,8,16,512]{4,3,2,1,0:T(8,128)(2,1)S(1)}, u32[]{:S(2)}) %copy-start) | copy-done | bytes 1572888
  17.1 45.7 %flow.1 = (bf16[8,48,2048]{2,1,0:T(8,128)(2,1)}, f32[3,64,512]{2,1,0:T(8,128)}) custom-call(bf16[4,3,8,16,512]{4,3,2,1,0:T(8,128)(2,1)} %copy-done, s32[64]{0:T(128)} %block.3, s32[64,512]{1,0:T(8,128)} %cell.3, f32[64,512]{1,0:T(8,128)} %rate.3, f32[64,512]{1,0:T(8,128)} %place.3, f32[3,64,512]{2,1,0:T(8,128)} %motion.3, ...), custom_call_target="tpu_custom_call" | custom-call | tf_op jit(solution)/shard_map/flow/pallas_call | solution.py:520
  62.8 0.0 copy-start.8
  62.8 3.8 %reshape.15 = bf16[8,3,8,2,2048]{4,3,2,1,0:T(2,128)(2,1)} reshape(bf16[8,48,2048]{2,1,0:T(8,128)(2,1)} %get-tuple-element.4) | data formatting | bytes 3145728 | tf_op jit(solution)/shard_map/reshape | solution.py:570
  66.6 0.0 copy-done.8
  66.6 0.7 %copy.16 = f32[3,64,512]{2,1,0:T(8,128)} copy(f32[3,64,512]{2,1,0:T(8,128)S(1)} %copy-done.8) | data formatting | bytes 786432
Async XLA Ops:
  0.6 1.0 %copy-start.1 = (f32[3,64,512]{2,1,0:T(8,128)S(1)}, f32[3,64,512]{2,1,0:T(8,128)}, u32[]{:S(2)}) copy-start(f32[3,64,512]{2,1,0:T(8,128)} %motion.3) | copy-start | bytes 1179652
  1.6 0.9 %copy-start.2 = (s32[64,512]{1,0:T(8,128)S(1)}, s32[64,512]{1,0:T(8,128)}, u32[]{:S(2)}) copy-start(s32[64,512]{1,0:T(8,128)} %cell.3) | copy-start | bytes 393220
  2.5 0.9 %copy-start.3 = (f32[64,512]{1,0:T(8,128)S(1)}, f32[64,512]{1,0:T(8,128)}, u32[]{:S(2)}) copy-start(f32[64,512]{1,0:T(8,128)} %rate.3) | copy-start | bytes 393220
  3.4 0.9 %copy-start.4 = (f32[64,512]{1,0:T(8,128)S(1)}, f32[64,512]{1,0:T(8,128)}, u32[]{:S(2)}) copy-start(f32[64,512]{1,0:T(8,128)} %place.3) | copy-start | bytes 393220
  4.3 1.0 %copy-start.5 = (f32[3,64,512]{2,1,0:T(8,128)S(1)}, f32[3,64,512]{2,1,0:T(8,128)}, u32[]{:S(2)}) copy-start(f32[3,64,512]{2,1,0:T(8,128)} %seen.1) | copy-start | bytes 1179652
  5.3 0.9 %copy-start.6 = (f32[64,512]{1,0:T(8,128)S(1)}, f32[64,512]{1,0:T(8,128)}, u32[]{:S(2)}) copy-start(f32[64,512]{1,0:T(8,128)} %volume.1) | copy-start | bytes 393220
  6.2 0.7 copy-start.7
  15.9 1.1 %copy-start = (bf16[4,3,8,16,512]{4,3,2,1,0:T(8,128)(2,1)}, bf16[4,3,8,16,512]{4,3,2,1,0:T(8,128)(2,1)S(1)}, u32[]{:S(2)}) copy-start(bf16[4,3,8,16,512]{4,3,2,1,0:T(8,128)(2,1)S(1)} %deposit.1.folded) | copy-start | bytes 4718596
  62.8 3.8 %copy-start.8 = (f32[3,64,512]{2,1,0:T(8,128)S(1)}, f32[3,64,512]{2,1,0:T(8,128)}, u32[]{:S(2)}) copy-start(f32[3,64,512]{2,1,0:T(8,128)} %get-tuple-element.9) | copy-start | bytes 1179652

commit v2 on v1

v2 whole, which is shorter than its diff:
```python
import math

import jax
import jax.numpy as jnp
import ml_dtypes
import numpy as np
from jax import lax
from jax.experimental import pallas as pl
from jax.experimental.pallas import tpu as pltpu
from jax.sharding import PartitionSpec as P

NX = 2048
KX = 1024
NY = 512
CB = 256
PT = 512
TILES = 64
MODES = 8
ROWS = 8
STRIPS = 8
WIDTH = 3 * 2 * MODES
BLOCKS = ROWS * STRIPS
FOLD = NX // 4
KEPT = KX // 4
N_PX = 8
N_PZ = 8
SLABS = N_PX * N_PZ
TURN = 1.0 / (2.0 * math.pi)
COSINE = (
    1.0,
    -19.73920440673828,
    64.93911743164062,
    -85.45011138916016,
    60.16743087768555,
    -25.96688461303711,
    6.527706146240234,
)

time_step = 0.5
gravity = 0.8
viscosity = 0.0001

f32 = jnp.float32
bf16 = jnp.bfloat16
VMEM = pl.BlockSpec(memory_space=pltpu.VMEM)
SMEM = pl.BlockSpec(memory_space=pltpu.SMEM)
ANY = pl.BlockSpec(memory_space=pl.ANY)


def wave_tables():
    x = np.arange(FOLD, dtype=np.int64)[None, :, None]
    k = (
        4 * np.arange(KEPT, dtype=np.int64)[None, None, :]
        + np.arange(4, dtype=np.int64)[:, None, None]
        - KX // 2
    )
    angle = np.mod(k * x, NX) * (2.0 * math.pi / NX)
    table = np.stack([np.cos(angle), np.sin(angle)], axis=1) / math.sqrt(NX)
    return table.astype(np.float32).astype(ml_dtypes.bfloat16)


def lane_order():
    perm = np.zeros((128, 128), np.float32)
    lanes = np.arange(128)
    perm[4 * (lanes % 32) + lanes // 32, lanes] = 1.0
    return np.concatenate([perm, perm], axis=0).astype(ml_dtypes.bfloat16)


def cosine_turns(turns):
    part = turns - jnp.round(turns)
    square = part * part
    value = jnp.full_like(square, COSINE[-1])
    for term in COSINE[-2::-1]:
        value = value * square + term
    return value


def one_hot_cells(cell_row):
    cells = jnp.broadcast_to(cell_row.astype(f32), (16, PT)).astype(bf16)
    lines = lax.broadcasted_iota(jnp.int32, (16, PT), 0).astype(f32).astype(bf16)
    one, zero = jnp.ones((16, PT), bf16), jnp.zeros((16, PT), bf16)
    return jnp.concatenate(
        [jnp.where(cells == lines + jnp.asarray(16 * i, bf16), one, zero) for i in range(16)],
        axis=0,
    )


def mode_turns(group):
    line = lax.broadcasted_iota(jnp.int32, (16, PT), 0)
    wave = (group * MODES + line % 8 + 1).astype(f32)
    shift = (line // 8).astype(f32) * 0.25
    return wave, shift


def swap_lanes(parts):
    return [
        jnp.concatenate([part[:, 32 * i : 32 * i + 32] for part in parts], axis=1)
        for i in range(4)
    ]


def dot(a, b):
    return lax.dot_general(a, b, (((1,), (0,)), ((), ())), preferred_element_type=f32)


def dot_t(a, b):
    return lax.dot_general(a, b, (((1,), (1,)), ((), ())), preferred_element_type=f32)


def block_fold(blocks_line):
    rows = lax.broadcasted_iota(jnp.int32, (128, 256), 0)
    lanes = lax.broadcasted_iota(jnp.int32, (128, 256), 1)
    q, s, r, y = rows // 32, (rows // 16) % 2, (rows // 8) % 2, rows % 8
    z = (lanes // TILES) % 2
    tile_block = jnp.broadcast_to(
        jnp.concatenate([blocks_line] * 4, axis=1), (128, 256)
    )
    strip = tile_block & 7
    turn = (q * (strip >> 1) + r - z + 4) & 3
    value = jnp.where(turn == 0, 1.0, jnp.where(turn == 2, -1.0, 0.0))
    here = ((tile_block >> 3) == y) & ((strip & 1) == s)
    return jnp.where(here, value, 0.0).astype(bf16)


def flow_kernel(
    block,
    block_line,
    eigenvalues,
    cell_any,
    place_any,
    volume_any,
    rate_any,
    motion_any,
    seen_any,
    tables_any,
    order_any,
    fluid_any,
    basis_any,
    inverse_any,
    planes_any,
    updated_any,
    cell,
    place,
    volume,
    rate,
    motion,
    seen,
    tables,
    order,
    fluid,
    basis,
    inverse,
    shares,
    folded,
    cell_hot,
    phases,
    split_basis,
    split_inverse,
    damping,
    ordered,
    forward_send,
    forward_recv,
    back_send,
    back_recv,
    planes,
    planes_out,
    blocks,
    part,
    part_send,
    part_recv,
    updated,
    load_sem,
    store_sem,
    own_sem,
    send_sem,
    recv_sem,
    part_send_sem,
    part_recv_sem,
):
    grp = lax.axis_index("grp")
    px = lax.axis_index("px")
    pz = lax.axis_index("pz")
    me = px * N_PZ + pz

    def peer(step):
        return lax.rem(px + step // N_PZ, N_PX), lax.rem(pz + lax.rem(step, N_PZ), N_PZ)

    sources = (cell_any, place_any, volume_any, rate_any, motion_any, seen_any)
    sources += (tables_any, order_any, fluid_any, basis_any, inverse_any)
    targets = (cell, place, volume, rate, motion, seen)
    targets += (tables, order, fluid, basis, inverse)
    loads = [
        pltpu.make_async_copy(source, target, load_sem.at[i])
        for i, (source, target) in enumerate(zip(sources, targets))
    ]
    for load in loads:
        load.start()

    barrier = pltpu.get_barrier_semaphore()

    def greet(step, carry):
        a, b = peer(step)
        pl.semaphore_signal(barrier, inc=1, device_id={"px": a, "pz": b})
        return carry

    pl.semaphore_signal(barrier, inc=1, device_id={"grp": 1 - grp})
    lax.fori_loop(1, SLABS, greet, 0)

    selection = block_fold(block_line[...])
    wave, shift = mode_turns(grp)
    for load in loads[:6]:
        load.wait()

    def deposit(turn, carry):
        first = pl.multiple_of(turn * 8, 8)
        here = pl.ds(first, 8)
        cells = cell[here, :]
        amount = volume[here, :]
        scale = amount * rate[here, :]
        angle = place[here, :] * TURN
        drags = [scale * (seen[c, here, :] - motion[c, here, :]) for c in range(3)]
        drags[1] = drags[1] - gravity * amount
        for i in range(8):
            phase = cosine_turns(
                wave * jnp.broadcast_to(angle[i : i + 1, :], (16, PT)) + shift
            )
            phases[first + i] = phase
            payload = jnp.concatenate(
                [
                    (phase * jnp.broadcast_to(drags[c][i : i + 1, :], (16, PT))).astype(bf16)
                    for c in range(3)
                ],
                axis=0,
            )
            share = dot_t(payload, one_hot_cells(cells[i : i + 1, :]))
            target = pl.ds(pl.multiple_of((first + i) * WIDTH, WIDTH), WIDTH)
            for h in range(2):
                shares[h, target, :] = share[:, 128 * h : 128 * h + 128]
        return carry

    lax.fori_loop(0, TILES // 8, deposit, 0)

    def fold(c):
        for m in range(MODES):
            high, low = [], []
            for z in range(2):
                halves = [
                    shares[h, pl.ds(c * 16 + z * 8 + m, TILES, stride=WIDTH), :]
                    for h in range(2)
                ]
                value = jnp.concatenate(halves, axis=1)
                top = value.astype(bf16)
                high.append(top)
                low.append((value - top.astype(f32)).astype(bf16))
            sums = dot(selection, jnp.concatenate(high + low, axis=0))
            for q in range(4):
                for s in range(2):
                    first = q * 32 + s * 16
                    folded[q, m * 16 : m * 16 + 16, 256 * s : 256 * s + 256] = sums[
                        first : first + 16, :
                    ].astype(bf16)

    def forward(c):
        classes = []
        for q in range(4):
            even = dot(folded[q], tables[q, 0]).reshape(MODES, 2, ROWS, KEPT)
            odd = dot(folded[q], tables[q, 1]).reshape(MODES, 2, ROWS, KEPT)
            re = even[:, 0] + odd[:, 1]
            im = even[:, 1] - odd[:, 0]
            classes.append(
                jnp.concatenate([re, im], axis=1).reshape(MODES * 16, KEPT)
            )
        for h in range(2):
            chunks = swap_lanes([item[:, 128 * h : 128 * h + 128] for item in classes])
            for i in range(4):
                first = (4 * h + i) * 128
                forward_send[c, :, :, first : first + 128] = (
                    chunks[i].astype(bf16).reshape(MODES, 16, 128)
                )

    def forward_start(c):
        def send(step, carry):
            a, b = peer(step)
            pltpu.make_async_remote_copy(
                forward_send.at[c, b, :, pl.ds(pl.multiple_of(a * 128, 128), 128)],
                forward_recv.at[c, me],
                send_sem.at[c],
                recv_sem.at[c],
                device_id={"px": a, "pz": b},
            ).start()
            return carry

        pltpu.make_async_copy(
            forward_send.at[c, pz, :, pl.ds(pl.multiple_of(px * 128, 128), 128)],
            forward_recv.at[c, me],
            own_sem.at[c],
        ).start()
        lax.fori_loop(1, SLABS, send, 0)

    def back_start(c):
        def send(step, carry):
            a, b = peer(step)
            pltpu.make_async_remote_copy(
                back_send.at[c, a * N_PZ + b],
                back_recv.at[c, pz, :, pl.ds(pl.multiple_of(px * 128, 128), 128)],
                send_sem.at[3 + c],
                recv_sem.at[3 + c],
                device_id={"px": a, "pz": b},
            ).start()
            return carry

        pltpu.make_async_copy(
            back_send.at[c, me],
            back_recv.at[c, pz, :, pl.ds(pl.multiple_of(px * 128, 128), 128)],
            own_sem.at[3 + c],
        ).start()
        lax.fori_loop(1, SLABS, send, 0)

    def exchange_wait(index):
        blocks_in = forward_recv.at[0, pl.ds(0, SLABS - 1)]
        pltpu.make_async_remote_copy(
            blocks_in,
            blocks_in,
            send_sem.at[index],
            recv_sem.at[index],
            device_id={"px": px, "pz": pz},
        ).wait_recv()
        own = forward_recv.at[0, 0]
        pltpu.make_async_copy(own, own, own_sem.at[index]).wait()

    def sent_wait(index):
        blocks_out = forward_recv.at[0, pl.ds(0, SLABS - 1)]
        pltpu.make_async_remote_copy(
            blocks_out,
            blocks_out,
            send_sem.at[index],
            recv_sem.at[index],
            device_id={"px": px, "pz": pz},
        ).wait_send()

    fold(0)
    for load in loads[6:]:
        load.wait()
    forward(0)
    pl.semaphore_wait(barrier, SLABS)
    forward_start(0)
    for c in range(1, 3):
        fold(c)
        forward(c)
        forward_start(c)

    for matrix, split in ((basis, split_basis), (inverse, split_inverse)):
        high = matrix[...].astype(bf16)
        split[0] = high
        split[1] = (matrix[...] - high.astype(f32)).astype(bf16)
    lane = lax.broadcasted_iota(jnp.int32, (1, 128), 1)
    stream = px * 128 + 4 * (lane % 32) + lane // 32 - KX // 2
    stream = stream.astype(f32) * 0.5
    span = (grp * MODES + pz + 1).astype(f32)
    square = stream * stream + span * span
    column = jnp.transpose(jnp.broadcast_to(eigenvalues[...], (128, NY)))
    damping[...] = 1.0 / (1.0 + viscosity * (column + square))
    for c in range(3):
        for r in range(2):
            state = fluid[pl.ds(c * 2 + r, NY, stride=6), :]
            high = state.astype(bf16)
            low = (state - high.astype(f32)).astype(bf16)
            ordered[c, :, 128 * r : 128 * r + 128] = dot(
                jnp.concatenate([high, low], axis=1), order[...]
            )

    def make_hot(turn, carry):
        first = pl.multiple_of(turn * 8, 8)
        cells = cell[pl.ds(first, 8), :]
        for i in range(8):
            cell_hot[first + i] = one_hot_cells(cells[i : i + 1, :])
        return carry

    lax.fori_loop(0, TILES // 8, make_hot, 0)

    def apply(split, value):
        high = value.astype(bf16)
        low = (value - high.astype(f32)).astype(bf16)
        return dot(split[0], high) + (dot(split[0], low) + dot(split[1], high))

    for c in range(3):
        exchange_wait(c)
        forcing = forward_recv[c].astype(f32)
        force = jnp.concatenate(
            [forcing[:, 8 * r : 8 * r + 8, :].reshape(NY, 128) for r in range(2)], axis=1
        )
        modal = apply(split_inverse, ordered[c] + time_step * force)
        damp = damping[...]
        solved = apply(split_basis, modal * jnp.concatenate([damp, damp], axis=1))
        back_send[c] = jnp.concatenate(
            [solved[:, 128 * r : 128 * r + 128].reshape(SLABS, ROWS, 128) for r in range(2)],
            axis=1,
        ).astype(bf16)
        back_start(c)

    def backward(c):
        halves = []
        for h in range(2):
            parts = [
                back_recv[c, :, :, (4 * h + i) * 128 : (4 * h + i) * 128 + 128].reshape(
                    MODES * 16, 128
                )
                for i in range(4)
            ]
            halves.append(swap_lanes(parts))
        re, im = [], []
        for q in range(4):
            rows = jnp.concatenate([halves[0][q], halves[1][q]], axis=1)
            even = dot_t(rows, tables[q, 0]).reshape(MODES, 2, ROWS, FOLD)
            odd = dot_t(rows, tables[q, 1]).reshape(MODES, 2, ROWS, FOLD)
            re.append(even[:, 0] - odd[:, 1])
            im.append(odd[:, 0] + even[:, 1])
        sums = (re[0] + re[2], im[0] + im[2])
        lefts = (re[0] - re[2], im[0] - im[2])
        others = (re[1] + re[3], im[1] + im[3])
        rights = (im[3] - im[1], re[1] - re[3])
        results = (
            (sums[0] + others[0], sums[1] + others[1]),
            (lefts[0] + rights[0], lefts[1] + rights[1]),
            (sums[0] - others[0], sums[1] - others[1]),
            (lefts[0] - rights[0], lefts[1] - rights[1]),
        )
        for j in range(4):
            for r in range(2):
                for m in range(MODES):
                    for t in range(4):
                        planes[
                            pl.ds(m * 32 + (4 * j + t) * 2 + r, ROWS, stride=MODES * 32), :
                        ] = results[j][r][m, :, 128 * t : 128 * t + 128]

        def one_row(y, carry):
            first = pl.multiple_of(y * MODES * 32, MODES * 32)
            planes_out[y, c] = planes[pl.ds(first, MODES * 32), :].astype(bf16)
            for s in range(STRIPS):
                for h in range(2):
                    pair = [
                        planes[pl.ds(first + (2 * s + h) * 2 + r, MODES, stride=32), :]
                        for r in range(2)
                    ]
                    blocks[c, y * STRIPS + s, :, 128 * h : 128 * h + 128] = jnp.concatenate(
                        pair, axis=0
                    ).astype(bf16)
            return carry

        lax.fori_loop(0, ROWS, one_row, 0)

    def part_copy(which, turn):
        c, count = (0, 2) if which == 0 else (2, 1)
        here = pl.ds(pl.multiple_of(turn * 16, 16), 16)
        return pltpu.make_async_remote_copy(
            part_send.at[pl.ds(c, count), here, :],
            part_recv.at[pl.ds(c, count), here, :],
            part_send_sem.at[which, turn],
            part_recv_sem.at[which, turn],
            device_id={"grp": 1 - grp},
        )

    def sample(which):
        components = (0, 1) if which == 0 else (2,)

        def sixteen_tiles(turn, carry):
            for half in range(2):
                first = pl.multiple_of(turn * 16 + 8 * half, 8)
                here = pl.ds(first, 8)
                lines = [[] for c in components]
                for i in range(8):
                    own_block = block[first + i]
                    rows = jnp.concatenate([blocks[c, own_block] for c in components], axis=0)
                    picked = dot(rows, cell_hot[first + i])
                    phase = phases[first + i]
                    for n in range(len(components)):
                        lines[n].append(
                            jnp.sum(
                                picked[16 * n : 16 * n + 16, :] * phase, axis=0, keepdims=True
                            )
                        )
                for n, c in enumerate(components):
                    part[c, here, :] = jnp.concatenate(lines[n], axis=0)
            here = pl.ds(pl.multiple_of(turn * 16, 16), 16)
            for c in components:
                part_send[c, here, :] = part[c, here, :].astype(bf16)
            part_copy(which, turn).start()
            return carry

        lax.fori_loop(0, TILES // 16, sixteen_tiles, 0)

    def update(which):
        components = (0, 1) if which == 0 else (2,)

        def sixteen_tiles(turn, carry):
            part_copy(which, turn).wait()
            here = pl.ds(pl.multiple_of(turn * 16, 16), 16)
            for c in components:
                fluid_at = part_send[c, here, :].astype(f32) + part_recv[c, here, :].astype(f32)
                old = motion[c, here, :]
                new = old + time_step * rate[here, :] * (fluid_at - old)
                updated[c, here, :] = new - time_step * gravity if c == 1 else new
            return carry

        lax.fori_loop(0, TILES // 16, sixteen_tiles, 0)

    stores = []

    def store(source, target):
        stores.append(pltpu.make_async_copy(source, target, store_sem.at[len(stores)]))
        stores[-1].start()

    exchange_wait(3)
    backward(0)
    store(planes_out.at[:, 0], planes_any.at[:, 0])
    exchange_wait(4)
    backward(1)
    store(planes_out.at[:, 1], planes_any.at[:, 1])
    sample(0)
    exchange_wait(5)
    backward(2)
    store(planes_out.at[:, 2], planes_any.at[:, 2])
    sample(1)
    update(0)
    store(updated.at[pl.ds(0, 2)], updated_any.at[pl.ds(0, 2)])
    update(1)
    store(updated.at[pl.ds(2, 1)], updated_any.at[pl.ds(2, 1)])
    for index in range(6):
        sent_wait(index)
    for item in stores:
        item.wait()


def on_device(
    cell_index,
    block_index,
    volume,
    response_rate,
    spanwise_position,
    particle_velocity,
    seen_velocity,
    fluid_velocity,
    eigen_basis,
    eigen_inverse,
    eigenvalues,
):
    tables = jnp.asarray(wave_tables())
    order = jnp.asarray(lane_order())
    particles = ((TILES, PT), f32)
    vectors = ((3, TILES, PT), f32)
    scratch = (
        ((TILES, PT), jnp.int32),
        particles,
        particles,
        particles,
        vectors,
        vectors,
        (tables.shape, bf16),
        (order.shape, bf16),
        ((NY * 6, 128), f32),
        ((NY, NY), f32),
        ((NY, NY), f32),
        ((2, TILES * WIDTH, 128), f32),
        ((4, MODES * 16, FOLD), bf16),
        ((TILES, CB, PT), bf16),
        ((TILES, 16, PT), f32),
        ((2, NY, NY), bf16),
        ((2, NY, NY), bf16),
        ((NY, 128), f32),
        ((3, NY, 256), f32),
        ((3, MODES, 16, KX), bf16),
        ((3, SLABS, 16, 128), bf16),
        ((3, SLABS, 16, 128), bf16),
        ((3, MODES, 16, KX), bf16),
        ((ROWS * MODES * 32, 128), f32),
        ((ROWS, 3, MODES * 32, 128), bf16),
        ((3, BLOCKS, 16, CB), bf16),
        vectors,
        ((3, TILES, PT), bf16),
        ((3, TILES, PT), bf16),
        vectors,
    )
    planes, updated = pl.pallas_call(
        flow_kernel,
        out_shape=(
            jax.ShapeDtypeStruct((ROWS, 3, MODES * 32, 128), bf16),
            jax.ShapeDtypeStruct((3, TILES, PT), f32),
        ),
        in_specs=[SMEM, VMEM, VMEM] + [ANY] * 11,
        out_specs=(ANY, ANY),
        scratch_shapes=[pltpu.VMEM(*item) for item in scratch]
        + [
            pltpu.SemaphoreType.DMA((11,)),
            pltpu.SemaphoreType.DMA((5,)),
            pltpu.SemaphoreType.DMA((6,)),
            pltpu.SemaphoreType.DMA((6,)),
            pltpu.SemaphoreType.DMA((6,)),
            pltpu.SemaphoreType.DMA((2, TILES // 16)),
            pltpu.SemaphoreType.DMA((2, TILES // 16)),
        ],
        compiler_params=pltpu.CompilerParams(
            collective_id=0, has_side_effects=True, vmem_limit_bytes=58 * 2**20
        ),
        name="flow",
    )(
        block_index,
        block_index.reshape(1, TILES),
        eigenvalues.reshape(1, NY),
        cell_index,
        spanwise_position,
        volume,
        response_rate,
        particle_velocity,
        seen_velocity,
        tables,
        order,
        fluid_velocity.reshape(NY * 6, 128),
        eigen_basis,
        eigen_inverse,
    )
    planes = planes.reshape(ROWS, 3, MODES, 16, 2, 128)
    planes = jnp.transpose(planes, (0, 1, 2, 4, 3, 5)).reshape(ROWS, 3, MODES, 2, NX)
    return planes, updated


def solution(mesh):
    in_specs = (
        P(("px", "pz"), None),
        P(("px", "pz")),
        P(("px", "pz"), None),
        P(("px", "pz"), None),
        P(("px", "pz"), None),
        P(None, ("px", "pz"), None),
        P(None, ("px", "pz"), None),
        P(None, None, ("grp", "pz"), None, "px"),
        P(),
        P(),
        P(),
    )
    out_specs = (P(("px", "pz"), None, "grp", None, None), P(None, ("px", "pz"), None))
    return jax.shard_map(
        on_device, mesh=mesh, in_specs=in_specs, out_specs=out_specs, check_vma=False
    )
```

time: 67.7 us -> 55.3 us (0.82)
  local copies, waits for them, and re-layouts: 11.9 us -> 4.97 us
  Pallas kernels: 54.7 us -> 49.5 us
    pallas_call x2 -> x1, Pallas kernels: 54.7 us -> 49.5 us  [on_device(): pl.pallas_call(flow_kernel, out_shape=(jax.ShapeDtypeStruct((ROWS, 3, MOD...]
    reshape x1 -> x0, local copies, waits for them, and re-layouts: 3.8 us -> none  [on_device(): return (planes.reshape(ROWS, 3, MODES, 2, NX), updated)]
    unnamed x19 -> x4, local copies, waits for them, and re-layouts: 8.14 us -> 4.97 us
where the time goes in v2:
time: 55.3 us; the launch traced here: 55.1 us
  Pallas kernels  49.5 us (90%)
  local copies, waits for them, and re-layouts  4.97 us (9%)
  between operations  0.65 us (1%)
    pallas_call x1, Pallas kernels, on_device(): pl.pallas_call(flow_kernel, out_shape=(jax.ShapeDtypeStruct((ROWS, 3, MOD...  49.5 us
    unnamed x4, local copies, waits for them, and re-layouts  4.97 us

profile of v2, /device:TPU:1, one launch (start us, length us, event | category | flops | bytes accessed | tf_op | source)
XLA Modules:
  0.0 55.1 jit_solution(7516007424540954985)
XLA Ops:
  0.6 49.5 %flow.1 = (bf16[8,3,256,128]{3,2,1,0:T(8,128)(2,1)}, f32[3,64,512]{2,1,0:T(8,128)}) custom-call(s32[64]{0:T(128)} %block.1, s32[1,64]{1,0:T(1,128)} %bitcast.11, f32[1,512]{1,0:T(1,128)} %bitcast.10, s32[64,512]{1,0:T(8,128)} %cell_any.1, f32[64,512]{1,0:T(8,128)} %place_any.1, f32[64,512]{1,0:T(8,128)} %volume_any.1, f32[64,512]{1,0:T(8,128)} %rate_any.1, ...), custom_call_target="tpu_custom_call" | custom-call | tf_op jit(solution)/shard_map/flow/pallas_call | solution.py:583
  50.1 0.0 copy-start
  50.1 4.2 %copy.18 = bf16[8,3,8,2,2048]{4,3,2,1,0:T(2,128)(2,1)} copy(bf16[8,3,8,2,2048]{4,3,2,1,0:T(2,128)(2,1)} %bitcast.8) | data formatting | bytes 3145728
  54.4 0.0 copy-done
  54.4 0.7 %copy.19 = f32[3,64,512]{2,1,0:T(8,128)} copy(f32[3,64,512]{2,1,0:T(8,128)S(1)} %copy-done) | data formatting | bytes 786432
Async XLA Ops:
  50.1 4.2 %copy-start = (f32[3,64,512]{2,1,0:T(8,128)S(1)}, f32[3,64,512]{2,1,0:T(8,128)}, u32[]{:S(2)}) copy-start(f32[3,64,512]{2,1,0:T(8,128)} %get-tuple-element.9) | copy-start | bytes 1179652

commit v3 on v2

--- a/solution.py
+++ b/solution.py
@@ -76,11 +76,11 @@
 
 
 def one_hot_cells(cell_row):
-    cells = jnp.broadcast_to(cell_row.astype(f32), (16, PT)).astype(bf16)
+    cells = jnp.broadcast_to((cell_row & 127).astype(f32), (16, PT)).astype(bf16)
     lines = lax.broadcasted_iota(jnp.int32, (16, PT), 0).astype(f32).astype(bf16)
     one, zero = jnp.ones((16, PT), bf16), jnp.zeros((16, PT), bf16)
     return jnp.concatenate(
-        [jnp.where(cells == lines + jnp.asarray(16 * i, bf16), one, zero) for i in range(16)],
+        [jnp.where(cells == lines + jnp.asarray(16 * i, bf16), one, zero) for i in range(8)],
         axis=0,
     )
 
@@ -152,7 +152,6 @@
     inverse,
     shares,
     folded,
-    cell_hot,
     phases,
     split_basis,
     split_inverse,
@@ -225,17 +224,18 @@
                 wave * jnp.broadcast_to(angle[i : i + 1, :], (16, PT)) + shift
             )
             phases[first + i] = phase
-            payload = jnp.concatenate(
-                [
-                    (phase * jnp.broadcast_to(drags[c][i : i + 1, :], (16, PT))).astype(bf16)
-                    for c in range(3)
-                ],
-                axis=0,
+            below = jnp.broadcast_to(cells[i : i + 1, :], (16, PT)) < 128
+            lower, upper = [], []
+            for c in range(3):
+                payload = phase * jnp.broadcast_to(drags[c][i : i + 1, :], (16, PT))
+                lower.append(jnp.where(below, payload, 0.0).astype(bf16))
+                upper.append(jnp.where(below, 0.0, payload).astype(bf16))
+            share = dot_t(
+                jnp.concatenate(lower + upper, axis=0), one_hot_cells(cells[i : i + 1, :])
             )
-            share = dot_t(payload, one_hot_cells(cells[i : i + 1, :]))
             target = pl.ds(pl.multiple_of((first + i) * WIDTH, WIDTH), WIDTH)
             for h in range(2):
-                shares[h, target, :] = share[:, 128 * h : 128 * h + 128]
+                shares[h, target, :] = share[WIDTH * h : WIDTH * h + WIDTH, :]
         return carry
 
     lax.fori_loop(0, TILES // 8, deposit, 0)
@@ -368,15 +368,6 @@
             ordered[c, :, 128 * r : 128 * r + 128] = dot(
                 jnp.concatenate([high, low], axis=1), order[...]
             )
-
-    def make_hot(turn, carry):
-        first = pl.multiple_of(turn * 8, 8)
-        cells = cell[pl.ds(first, 8), :]
-        for i in range(8):
-            cell_hot[first + i] = one_hot_cells(cells[i : i + 1, :])
-        return carry
-
-    lax.fori_loop(0, TILES // 8, make_hot, 0)
 
     def apply(split, value):
         high = value.astype(bf16)
@@ -449,60 +440,53 @@
 
         lax.fori_loop(0, ROWS, one_row, 0)
 
-    def part_copy(which, turn):
-        c, count = (0, 2) if which == 0 else (2, 1)
+    def part_copy(turn):
         here = pl.ds(pl.multiple_of(turn * 16, 16), 16)
         return pltpu.make_async_remote_copy(
-            part_send.at[pl.ds(c, count), here, :],
-            part_recv.at[pl.ds(c, count), here, :],
-            part_send_sem.at[which, turn],
-            part_recv_sem.at[which, turn],
+            part_send.at[:, here, :],
+            part_recv.at[:, here, :],
+            part_send_sem.at[turn],
+            part_recv_sem.at[turn],
             device_id={"grp": 1 - grp},
         )
 
-    def sample(which):
-        components = (0, 1) if which == 0 else (2,)
-
-        def sixteen_tiles(turn, carry):
-            for half in range(2):
-                first = pl.multiple_of(turn * 16 + 8 * half, 8)
-                here = pl.ds(first, 8)
-                lines = [[] for c in components]
-                for i in range(8):
-                    own_block = block[first + i]
-                    rows = jnp.concatenate([blocks[c, own_block] for c in components], axis=0)
-                    picked = dot(rows, cell_hot[first + i])
-                    phase = phases[first + i]
-                    for n in range(len(components)):
-                        lines[n].append(
-                            jnp.sum(
-                                picked[16 * n : 16 * n + 16, :] * phase, axis=0, keepdims=True
-                            )
-                        )
-                for n, c in enumerate(components):
-                    part[c, here, :] = jnp.concatenate(lines[n], axis=0)
-            here = pl.ds(pl.multiple_of(turn * 16, 16), 16)
-            for c in components:
-                part_send[c, here, :] = part[c, here, :].astype(bf16)
-            part_copy(which, turn).start()
-            return carry
-
-        lax.fori_loop(0, TILES // 16, sixteen_tiles, 0)
-
-    def update(which):
-        components = (0, 1) if which == 0 else (2,)
-
-        def sixteen_tiles(turn, carry):
-            part_copy(which, turn).wait()
-            here = pl.ds(pl.multiple_of(turn * 16, 16), 16)
-            for c in components:
-                fluid_at = part_send[c, here, :].astype(f32) + part_recv[c, here, :].astype(f32)
-                old = motion[c, here, :]
-                new = old + time_step * rate[here, :] * (fluid_at - old)
-                updated[c, here, :] = new - time_step * gravity if c == 1 else new
-            return carry
-
-        lax.fori_loop(0, TILES // 16, sixteen_tiles, 0)
+    def sample(turn, carry):
+        for half in range(2):
+            first = pl.multiple_of(turn * 16 + 8 * half, 8)
+            here = pl.ds(first, 8)
+            cells = cell[here, :]
+            lines = [[], [], []]
+            for i in range(8):
+                own_block = block[first + i]
+                rows = [blocks[c, own_block] for c in range(3)]
+                rows = jnp.concatenate(
+                    [item[:, :128] for item in rows] + [item[:, 128:] for item in rows], axis=0
+                )
+                both = dot(rows, one_hot_cells(cells[i : i + 1, :]))
+                below = jnp.broadcast_to(cells[i : i + 1, :], (WIDTH, PT)) < 128
+                picked = jnp.where(below, both[:WIDTH], both[WIDTH:])
+                phase = phases[first + i]
+                for c in range(3):
+                    lines[c].append(
+                        jnp.sum(picked[16 * c : 16 * c + 16, :] * phase, axis=0, keepdims=True)
+                    )
+            for c in range(3):
+                part[c, here, :] = jnp.concatenate(lines[c], axis=0)
+        here = pl.ds(pl.multiple_of(turn * 16, 16), 16)
+        for c in range(3):
+            part_send[c, here, :] = part[c, here, :].astype(bf16)
+        part_copy(turn).start()
+        return carry
+
+    def update(turn, carry):
+        part_copy(turn).wait()
+        here = pl.ds(pl.multiple_of(turn * 16, 16), 16)
+        for c in range(3):
+            fluid_at = part_send[c, here, :].astype(f32) + part_recv[c, here, :].astype(f32)
+            old = motion[c, here, :]
+            new = old + time_step * rate[here, :] * (fluid_at - old)
+            updated[c, here, :] = new - time_step * gravity if c == 1 else new
+        return carry
 
     stores = []
 
@@ -510,24 +494,28 @@
         stores.append(pltpu.make_async_copy(source, target, store_sem.at[len(stores)]))
         stores[-1].start()
 
-    exchange_wait(3)
-    backward(0)
-    store(planes_out.at[:, 0], planes_any.at[:, 0])
-    exchange_wait(4)
-    backward(1)
-    store(planes_out.at[:, 1], planes_any.at[:, 1])
-    sample(0)
-    exchange_wait(5)
-    backward(2)
-    store(planes_out.at[:, 2], planes_any.at[:, 2])
-    sample(1)
-    update(0)
-    store(updated.at[pl.ds(0, 2)], updated_any.at[pl.ds(0, 2)])
-    update(1)
-    store(updated.at[pl.ds(2, 1)], updated_any.at[pl.ds(2, 1)])
+    for c in range(3):
+        exchange_wait(3 + c)
+        backward(c)
+        store(planes_out.at[:, c], planes_any.at[:, c])
+    lax.fori_loop(0, TILES // 16, sample, 0)
+    lax.fori_loop(0, TILES // 16, update, 0)
+    store(updated, updated_any)
     for index in range(6):
         sent_wait(index)
     for item in stores:
+        item.wait()
+
+
+def deliver_kernel(planes_any, updated_any, planes_out, updated_out, sem):
+    copies = [
+        pltpu.make_async_copy(planes_any.at[pl.ds(2 * i, 2)], planes_out.at[pl.ds(2 * i, 2)], sem.at[i])
+        for i in range(4)
+    ]
+    copies.append(pltpu.make_async_copy(updated_any, updated_out, sem.at[4]))
+    for item in copies:
+        item.start()
+    for item in copies:
         item.wait()
 
 
@@ -562,7 +550,6 @@
         ((NY, NY), f32),
         ((2, TILES * WIDTH, 128), f32),
         ((4, MODES * 16, FOLD), bf16),
-        ((TILES, CB, PT), bf16),
         ((TILES, 16, PT), f32),
         ((2, NY, NY), bf16),
         ((2, NY, NY), bf16),
@@ -591,12 +578,12 @@
         scratch_shapes=[pltpu.VMEM(*item) for item in scratch]
         + [
             pltpu.SemaphoreType.DMA((11,)),
-            pltpu.SemaphoreType.DMA((5,)),
+            pltpu.SemaphoreType.DMA((4,)),
             pltpu.SemaphoreType.DMA((6,)),
             pltpu.SemaphoreType.DMA((6,)),
             pltpu.SemaphoreType.DMA((6,)),
-            pltpu.SemaphoreType.DMA((2, TILES // 16)),
-            pltpu.SemaphoreType.DMA((2, TILES // 16)),
+            pltpu.SemaphoreType.DMA((TILES // 16,)),
+            pltpu.SemaphoreType.DMA((TILES // 16,)),
         ],
         compiler_params=pltpu.CompilerParams(
             collective_id=0, has_side_effects=True, vmem_limit_bytes=58 * 2**20
@@ -618,6 +605,18 @@
         eigen_basis,
         eigen_inverse,
     )
+    planes, updated = pl.pallas_call(
+        deliver_kernel,
+        out_shape=(
+            jax.ShapeDtypeStruct(planes.shape, bf16),
+            jax.ShapeDtypeStruct(updated.shape, f32),
+        ),
+        in_specs=[ANY, ANY],
+        out_specs=(ANY, ANY),
+        scratch_shapes=[pltpu.SemaphoreType.DMA((5,))],
+        compiler_params=pltpu.CompilerParams(vmem_limit_bytes=58 * 2**20),
+        name="deliver",
+    )(planes, updated)
     planes = planes.reshape(ROWS, 3, MODES, 16, 2, 128)
     planes = jnp.transpose(planes, (0, 1, 2, 4, 3, 5)).reshape(ROWS, 3, MODES, 2, NX)
     return planes, updated

time: 55.3 us -> 106 us (1.92)
  Pallas kernels: 49.5 us -> 105 us
  local copies, waits for them, and re-layouts: 4.97 us -> 0 us
    pallas_call x0 -> x1, Pallas kernels: none -> 60.7 us  [on_device(): pl.pallas_call(deliver_kernel, out_shape=(jax.ShapeDtypeStruct(planes.sha...]
    unnamed x4 -> x0, local copies, waits for them, and re-layouts: 4.97 us -> none
    pallas_call x1, Pallas kernels: 49.5 us -> 44.8 us  [on_device(): pl.pallas_call(flow_kernel, out_shape=(jax.ShapeDtypeStruct((ROWS, 3, MOD...]
where the time goes in v3:
time: 106 us
  Pallas kernels  105 us (99%)
    pallas_call x1, Pallas kernels, on_device(): pl.pallas_call(deliver_kernel, out_shape=(jax.ShapeDtypeStruct(planes.sha...  60.7 us
    pallas_call x1, Pallas kernels, on_device(): pl.pallas_call(flow_kernel, out_shape=(jax.ShapeDtypeStruct((ROWS, 3, MOD...  44.8 us

profile of v3, /device:TPU:1, one launch (start us, length us, event | category | flops | bytes accessed | tf_op | source)
XLA Modules:
  0.0 106.1 jit_solution(12222024109314164713)
XLA Ops:
  0.6 44.8 %flow.1 = (bf16[8,3,256,128]{3,2,1,0:T(8,128)(2,1)}, f32[3,64,512]{2,1,0:T(8,128)}) custom-call(s32[64]{0:T(128)} %block.1, s32[1,64]{1,0:T(1,128)} %bitcast.10, f32[1,512]{1,0:T(1,128)} %bitcast.9, s32[64,512]{1,0:T(8,128)} %cell_any.1, f32[64,512]{1,0:T(8,128)} %place_any.1, f32[64,512]{1,0:T(8,128)} %volume_any.1, f32[64,512]{1,0:T(8,128)} %rate_any.1, ...), custom_call_target="tpu_custom_call" | custom-call | tf_op jit(solution)/shard_map/flow/pallas_call | solution.py:570
  45.4 60.7 %deliver.1 = (bf16[8,3,256,128]{3,2,1,0:T(8,128)(2,1)}, f32[3,64,512]{2,1,0:T(8,128)}) custom-call(bf16[8,3,256,128]{3,2,1,0:T(8,128)(2,1)} %get-tuple-element.6.planes_any, f32[3,64,512]{2,1,0:T(8,128)} %get-tuple-element.7.updated_any), custom_call_target="tpu_custom_call" | custom-call | tf_op jit(solution)/shard_map/deliver/pallas_call | solution.py:608

commit v4 on v3

--- a/solution.py
+++ b/solution.py
@@ -507,16 +507,21 @@
         item.wait()
 
 
-def deliver_kernel(planes_any, updated_any, planes_out, updated_out, sem):
-    copies = [
-        pltpu.make_async_copy(planes_any.at[pl.ds(2 * i, 2)], planes_out.at[pl.ds(2 * i, 2)], sem.at[i])
+def deliver_kernel(planes_any, updated_any, planes_out, updated_out, planes, updated, load_sem, store_sem):
+    pairs = [
+        (planes_any.at[pl.ds(2 * i, 2)], planes.at[pl.ds(2 * i, 2)], planes_out.at[pl.ds(2 * i, 2)])
         for i in range(4)
     ]
-    copies.append(pltpu.make_async_copy(updated_any, updated_out, sem.at[4]))
-    for item in copies:
-        item.start()
-    for item in copies:
-        item.wait()
+    pairs.append((updated_any, updated, updated_out))
+    loads = [pltpu.make_async_copy(a, b, load_sem.at[i]) for i, (a, b, c) in enumerate(pairs)]
+    stores = [pltpu.make_async_copy(b, c, store_sem.at[i]) for i, (a, b, c) in enumerate(pairs)]
+    for load in loads:
+        load.start()
+    for load, store in zip(loads, stores):
+        load.wait()
+        store.start()
+    for store in stores:
+        store.wait()
 
 
 def on_device(
@@ -613,7 +618,12 @@
         ),
         in_specs=[ANY, ANY],
         out_specs=(ANY, ANY),
-        scratch_shapes=[pltpu.SemaphoreType.DMA((5,))],
+        scratch_shapes=[
+            pltpu.VMEM(planes.shape, bf16),
+            pltpu.VMEM(updated.shape, f32),
+            pltpu.SemaphoreType.DMA((5,)),
+            pltpu.SemaphoreType.DMA((5,)),
+        ],
         compiler_params=pltpu.CompilerParams(vmem_limit_bytes=58 * 2**20),
         name="deliver",
     )(planes, updated)

time: 106 us -> 47.9 us (0.45)
  Pallas kernels: 105 us -> 47.1 us
    pallas_call x1, Pallas kernels: 60.7 us -> 2.35 us  [on_device(): pl.pallas_call(deliver_kernel, out_shape=(jax.ShapeDtypeStruct(planes.sha...]
where the time goes in v4:
time: 47.9 us; the launch traced here: 47.8 us
  Pallas kernels  47.1 us (98%)
  between operations  0.64 us (1%)
    pallas_call x1, Pallas kernels, on_device(): pl.pallas_call(flow_kernel, out_shape=(jax.ShapeDtypeStruct((ROWS, 3, MOD...  44.8 us
    pallas_call x1, Pallas kernels, on_device(): pl.pallas_call(deliver_kernel, out_shape=(jax.ShapeDtypeStruct(planes.sha...  2.35 us

profile of v4, /device:TPU:1, one launch (start us, length us, event | category | flops | bytes accessed | tf_op | source)
XLA Modules:
  0.0 47.8 jit_solution(3496799834071680754)
XLA Ops:
  0.6 44.8 %flow.1 = (bf16[8,3,256,128]{3,2,1,0:T(8,128)(2,1)}, f32[3,64,512]{2,1,0:T(8,128)}) custom-call(s32[64]{0:T(128)} %block.1, s32[1,64]{1,0:T(1,128)} %bitcast.10, f32[1,512]{1,0:T(1,128)} %bitcast.9, s32[64,512]{1,0:T(8,128)} %cell_any.1, f32[64,512]{1,0:T(8,128)} %place_any.1, f32[64,512]{1,0:T(8,128)} %volume_any.1, f32[64,512]{1,0:T(8,128)} %rate_any.1, ...), custom_call_target="tpu_custom_call" | custom-call | tf_op jit(solution)/shard_map/flow/pallas_call | solution.py:575
  45.4 2.3 %deliver.1 = (bf16[8,3,256,128]{3,2,1,0:T(8,128)(2,1)}, f32[3,64,512]{2,1,0:T(8,128)}) custom-call(bf16[8,3,256,128]{3,2,1,0:T(8,128)(2,1)} %get-tuple-element.6.planes_any, f32[3,64,512]{2,1,0:T(8,128)} %get-tuple-element.7.updated_any), custom_call_target="tpu_custom_call" | custom-call | tf_op jit(solution)/shard_map/deliver/pallas_call | solution.py:613

commit v5 on v2

--- a/solution.py
+++ b/solution.py
@@ -22,6 +22,7 @@
 BLOCKS = ROWS * STRIPS
 FOLD = NX // 4
 KEPT = KX // 4
+PASSES = ((0, 1), (2,))
 N_PX = 8
 N_PZ = 8
 SLABS = N_PX * N_PZ
@@ -43,8 +44,7 @@
 f32 = jnp.float32
 bf16 = jnp.bfloat16
 VMEM = pl.BlockSpec(memory_space=pltpu.VMEM)
-SMEM = pl.BlockSpec(memory_space=pltpu.SMEM)
-ANY = pl.BlockSpec(memory_space=pl.ANY)
+HBM = pl.BlockSpec(memory_space=pltpu.HBM)
 
 
 def wave_tables():
@@ -76,11 +76,11 @@
 
 
 def one_hot_cells(cell_row):
-    cells = jnp.broadcast_to(cell_row.astype(f32), (16, PT)).astype(bf16)
+    cells = jnp.broadcast_to((cell_row & 127).astype(f32), (16, PT)).astype(bf16)
     lines = lax.broadcasted_iota(jnp.int32, (16, PT), 0).astype(f32).astype(bf16)
     one, zero = jnp.ones((16, PT), bf16), jnp.zeros((16, PT), bf16)
     return jnp.concatenate(
-        [jnp.where(cells == lines + jnp.asarray(16 * i, bf16), one, zero) for i in range(16)],
+        [jnp.where(cells == lines + jnp.asarray(16 * i, bf16), one, zero) for i in range(8)],
         axis=0,
     )
 
@@ -123,9 +123,9 @@
 
 
 def flow_kernel(
-    block,
-    block_line,
-    eigenvalues,
+    block_any,
+    block_line_any,
+    eigenvalues_any,
     cell_any,
     place_any,
     volume_any,
@@ -137,8 +137,11 @@
     fluid_any,
     basis_any,
     inverse_any,
-    planes_any,
-    updated_any,
+    planes_out,
+    updated,
+    block,
+    block_line,
+    eigenvalues,
     cell,
     place,
     volume,
@@ -152,7 +155,6 @@
     inverse,
     shares,
     folded,
-    cell_hot,
     phases,
     split_basis,
     split_inverse,
@@ -163,14 +165,11 @@
     back_send,
     back_recv,
     planes,
-    planes_out,
     blocks,
     part,
     part_send,
     part_recv,
-    updated,
     load_sem,
-    store_sem,
     own_sem,
     send_sem,
     recv_sem,
@@ -186,9 +185,9 @@
         return lax.rem(px + step // N_PZ, N_PX), lax.rem(pz + lax.rem(step, N_PZ), N_PZ)
 
     sources = (cell_any, place_any, volume_any, rate_any, motion_any, seen_any)
-    sources += (tables_any, order_any, fluid_any, basis_any, inverse_any)
+    sources += (block_line_any, block_any, eigenvalues_any, tables_any, order_any, fluid_any, basis_any, inverse_any)
     targets = (cell, place, volume, rate, motion, seen)
-    targets += (tables, order, fluid, basis, inverse)
+    targets += (block_line, block, eigenvalues, tables, order, fluid, basis, inverse)
     loads = [
         pltpu.make_async_copy(source, target, load_sem.at[i])
         for i, (source, target) in enumerate(zip(sources, targets))
@@ -206,10 +205,10 @@
     pl.semaphore_signal(barrier, inc=1, device_id={"grp": 1 - grp})
     lax.fori_loop(1, SLABS, greet, 0)
 
+    wave, shift = mode_turns(grp)
+    for load in loads[:7]:
+        load.wait()
     selection = block_fold(block_line[...])
-    wave, shift = mode_turns(grp)
-    for load in loads[:6]:
-        load.wait()
 
     def deposit(turn, carry):
         first = pl.multiple_of(turn * 8, 8)
@@ -225,17 +224,18 @@
                 wave * jnp.broadcast_to(angle[i : i + 1, :], (16, PT)) + shift
             )
             phases[first + i] = phase
-            payload = jnp.concatenate(
-                [
-                    (phase * jnp.broadcast_to(drags[c][i : i + 1, :], (16, PT))).astype(bf16)
-                    for c in range(3)
-                ],
-                axis=0,
+            below = jnp.broadcast_to(cells[i : i + 1, :], (16, PT)) < 128
+            lower, upper = [], []
+            for c in range(3):
+                payload = phase * jnp.broadcast_to(drags[c][i : i + 1, :], (16, PT))
+                lower.append(jnp.where(below, payload, 0.0).astype(bf16))
+                upper.append(jnp.where(below, 0.0, payload).astype(bf16))
+            share = dot_t(
+                jnp.concatenate(lower + upper, axis=0), one_hot_cells(cells[i : i + 1, :])
             )
-            share = dot_t(payload, one_hot_cells(cells[i : i + 1, :]))
             target = pl.ds(pl.multiple_of((first + i) * WIDTH, WIDTH), WIDTH)
             for h in range(2):
-                shares[h, target, :] = share[:, 128 * h : 128 * h + 128]
+                shares[h, target, :] = share[WIDTH * h : WIDTH * h + WIDTH, :]
         return carry
 
     lax.fori_loop(0, TILES // 8, deposit, 0)
@@ -339,7 +339,7 @@
         ).wait_send()
 
     fold(0)
-    for load in loads[6:]:
+    for load in loads[7:]:
         load.wait()
     forward(0)
     pl.semaphore_wait(barrier, SLABS)
@@ -368,15 +368,6 @@
             ordered[c, :, 128 * r : 128 * r + 128] = dot(
                 jnp.concatenate([high, low], axis=1), order[...]
             )
-
-    def make_hot(turn, carry):
-        first = pl.multiple_of(turn * 8, 8)
-        cells = cell[pl.ds(first, 8), :]
-        for i in range(8):
-            cell_hot[first + i] = one_hot_cells(cells[i : i + 1, :])
-        return carry
-
-    lax.fori_loop(0, TILES // 8, make_hot, 0)
 
     def apply(split, value):
         high = value.astype(bf16)
@@ -449,53 +440,55 @@
 
         lax.fori_loop(0, ROWS, one_row, 0)
 
-    def part_copy(which, turn):
-        c, count = (0, 2) if which == 0 else (2, 1)
-        here = pl.ds(pl.multiple_of(turn * 16, 16), 16)
+    def part_copy(group, turn):
+        here = (pl.ds(group[0], len(group)), pl.ds(pl.multiple_of(turn * 16, 16), 16))
         return pltpu.make_async_remote_copy(
-            part_send.at[pl.ds(c, count), here, :],
-            part_recv.at[pl.ds(c, count), here, :],
-            part_send_sem.at[which, turn],
-            part_recv_sem.at[which, turn],
+            part_send.at[here],
+            part_recv.at[here],
+            part_send_sem.at[group[0], turn],
+            part_recv_sem.at[group[0], turn],
             device_id={"grp": 1 - grp},
         )
 
-    def sample(which):
-        components = (0, 1) if which == 0 else (2,)
-
+    def sample(group):
         def sixteen_tiles(turn, carry):
             for half in range(2):
                 first = pl.multiple_of(turn * 16 + 8 * half, 8)
                 here = pl.ds(first, 8)
-                lines = [[] for c in components]
+                cells = cell[here, :]
+                lines = [[] for c in group]
+                width = 16 * len(group)
                 for i in range(8):
                     own_block = block[first + i]
-                    rows = jnp.concatenate([blocks[c, own_block] for c in components], axis=0)
-                    picked = dot(rows, cell_hot[first + i])
+                    rows = [blocks[c, own_block] for c in group]
+                    rows = jnp.concatenate(
+                        [item[:, :128] for item in rows] + [item[:, 128:] for item in rows], axis=0
+                    )
+                    both = dot(rows, one_hot_cells(cells[i : i + 1, :]))
+                    below = jnp.broadcast_to(cells[i : i + 1, :], (width, PT)) < 128
+                    picked = jnp.where(below, both[:width], both[width:])
                     phase = phases[first + i]
-                    for n in range(len(components)):
+                    for n in range(len(group)):
                         lines[n].append(
                             jnp.sum(
                                 picked[16 * n : 16 * n + 16, :] * phase, axis=0, keepdims=True
                             )
                         )
-                for n, c in enumerate(components):
+                for n, c in enumerate(group):
                     part[c, here, :] = jnp.concatenate(lines[n], axis=0)
             here = pl.ds(pl.multiple_of(turn * 16, 16), 16)
-            for c in components:
+            for c in group:
                 part_send[c, here, :] = part[c, here, :].astype(bf16)
-            part_copy(which, turn).start()
+            part_copy(group, turn).start()
             return carry
 
         lax.fori_loop(0, TILES // 16, sixteen_tiles, 0)
 
-    def update(which):
-        components = (0, 1) if which == 0 else (2,)
-
+    def update(group):
         def sixteen_tiles(turn, carry):
-            part_copy(which, turn).wait()
+            part_copy(group, turn).wait()
             here = pl.ds(pl.multiple_of(turn * 16, 16), 16)
-            for c in components:
+            for c in group:
                 fluid_at = part_send[c, here, :].astype(f32) + part_recv[c, here, :].astype(f32)
                 old = motion[c, here, :]
                 new = old + time_step * rate[here, :] * (fluid_at - old)
@@ -504,31 +497,29 @@
 
         lax.fori_loop(0, TILES // 16, sixteen_tiles, 0)
 
-    stores = []
-
-    def store(source, target):
-        stores.append(pltpu.make_async_copy(source, target, store_sem.at[len(stores)]))
-        stores[-1].start()
-
-    exchange_wait(3)
-    backward(0)
-    store(planes_out.at[:, 0], planes_any.at[:, 0])
-    exchange_wait(4)
-    backward(1)
-    store(planes_out.at[:, 1], planes_any.at[:, 1])
-    sample(0)
-    exchange_wait(5)
-    backward(2)
-    store(planes_out.at[:, 2], planes_any.at[:, 2])
-    sample(1)
-    update(0)
-    store(updated.at[pl.ds(0, 2)], updated_any.at[pl.ds(0, 2)])
-    update(1)
-    store(updated.at[pl.ds(2, 1)], updated_any.at[pl.ds(2, 1)])
+    for group in PASSES:
+        for c in group:
+            exchange_wait(3 + c)
+            backward(c)
+        sample(group)
+    for group in PASSES:
+        update(group)
     for index in range(6):
         sent_wait(index)
-    for item in stores:
-        item.wait()
+
+
+def deliver_kernel(planes, updated, planes_out, updated_out, sem):
+    stores = [
+        pltpu.make_async_copy(
+            planes.at[pl.ds(2 * i, 2)], planes_out.at[pl.ds(2 * i, 2)], sem.at[i]
+        )
+        for i in range(4)
+    ]
+    stores.append(pltpu.make_async_copy(updated, updated_out, sem.at[4]))
+    for store in stores:
+        store.start()
+    for store in stores:
+        store.wait()
 
 
 def on_device(
@@ -549,6 +540,8 @@
     particles = ((TILES, PT), f32)
     vectors = ((3, TILES, PT), f32)
     scratch = (
+        ((1, TILES), jnp.int32),
+        ((1, NY), f32),
         ((TILES, PT), jnp.int32),
         particles,
         particles,
@@ -562,7 +555,6 @@
         ((NY, NY), f32),
         ((2, TILES * WIDTH, 128), f32),
         ((4, MODES * 16, FOLD), bf16),
-        ((TILES, CB, PT), bf16),
         ((TILES, 16, PT), f32),
         ((2, NY, NY), bf16),
         ((2, NY, NY), bf16),
@@ -573,12 +565,10 @@
         ((3, SLABS, 16, 128), bf16),
         ((3, MODES, 16, KX), bf16),
         ((ROWS * MODES * 32, 128), f32),
-        ((ROWS, 3, MODES * 32, 128), bf16),
         ((3, BLOCKS, 16, CB), bf16),
         vectors,
         ((3, TILES, PT), bf16),
         ((3, TILES, PT), bf16),
-        vectors,
     )
     planes, updated = pl.pallas_call(
         flow_kernel,
@@ -586,23 +576,25 @@
             jax.ShapeDtypeStruct((ROWS, 3, MODES * 32, 128), bf16),
             jax.ShapeDtypeStruct((3, TILES, PT), f32),
         ),
-        in_specs=[SMEM, VMEM, VMEM] + [ANY] * 11,
-        out_specs=(ANY, ANY),
-        scratch_shapes=[pltpu.VMEM(*item) for item in scratch]
+        in_specs=[HBM] * 14,
+        out_specs=(VMEM, VMEM),
+        scratch_shapes=[pltpu.SMEM((TILES,), jnp.int32)]
+        + [pltpu.VMEM(*item) for item in scratch]
         + [
-            pltpu.SemaphoreType.DMA((11,)),
-            pltpu.SemaphoreType.DMA((5,)),
+            pltpu.SemaphoreType.DMA((14,)),
             pltpu.SemaphoreType.DMA((6,)),
             pltpu.SemaphoreType.DMA((6,)),
             pltpu.SemaphoreType.DMA((6,)),
-            pltpu.SemaphoreType.DMA((2, TILES // 16)),
-            pltpu.SemaphoreType.DMA((2, TILES // 16)),
+            pltpu.SemaphoreType.DMA((3, TILES // 16)),
+            pltpu.SemaphoreType.DMA((3, TILES // 16)),
         ],
         compiler_params=pltpu.CompilerParams(
-            collective_id=0, has_side_effects=True, vmem_limit_bytes=58 * 2**20
+            collective_id=0, has_side_effects=True, vmem_limit_bytes=36 * 2**20
         ),
         name="flow",
-    )(
+    )(*(
+        pltpu.with_memory_space_constraint(item, pltpu.HBM)
+        for item in (
         block_index,
         block_index.reshape(1, TILES),
         eigenvalues.reshape(1, NY),
@@ -617,7 +609,20 @@
         fluid_velocity.reshape(NY * 6, 128),
         eigen_basis,
         eigen_inverse,
-    )
+            )
+    ))
+    planes, updated = pl.pallas_call(
+        deliver_kernel,
+        out_shape=(
+            jax.ShapeDtypeStruct(planes.shape, bf16),
+            jax.ShapeDtypeStruct((3, TILES, PT), f32),
+        ),
+        in_specs=[VMEM, VMEM],
+        out_specs=(HBM, HBM),
+        scratch_shapes=[pltpu.SemaphoreType.DMA((5,))],
+        compiler_params=pltpu.CompilerParams(vmem_limit_bytes=8 * 2**20),
+        name="deliver",
+    )(planes, updated)
     planes = planes.reshape(ROWS, 3, MODES, 16, 2, 128)
     planes = jnp.transpose(planes, (0, 1, 2, 4, 3, 5)).reshape(ROWS, 3, MODES, 2, NX)
     return planes, updated

time: 55.3 us -> 44.2 us (0.80)
  Pallas kernels: 49.5 us -> 43.4 us
  local copies, waits for them, and re-layouts: 4.97 us -> 0 us
    pallas_call x1, Pallas kernels: 49.5 us -> 42.1 us  [on_device(): pl.pallas_call(flow_kernel, out_shape=(jax.ShapeDtypeStruct((ROWS, 3, MOD...]
    unnamed x4 -> x0, local copies, waits for them, and re-layouts: 4.97 us -> none
    pallas_call x0 -> x1, Pallas kernels: none -> 1.31 us  [on_device(): pl.pallas_call(deliver_kernel, out_shape=(jax.ShapeDtypeStruct(planes.sha...]
where the time goes in v5:
time: 44.2 us; the launch traced here: 44.1 us
  Pallas kernels  43.4 us (98%)
  between operations  0.64 us (1%)
    pallas_call x1, Pallas kernels, on_device(): pl.pallas_call(flow_kernel, out_shape=(jax.ShapeDtypeStruct((ROWS, 3, MOD...  42.1 us
    pallas_call x1, Pallas kernels, on_device(): pl.pallas_call(deliver_kernel, out_shape=(jax.ShapeDtypeStruct(planes.sha...  1.31 us

profile of v5, /device:TPU:1, one launch (start us, length us, event | category | flops | bytes accessed | tf_op | source)
XLA Modules:
  0.0 44.1 jit_solution(17675584975927536306)
XLA Ops:
  0.6 42.1 %flow.1 = (bf16[8,3,256,128]{3,2,1,0:T(8,128)(2,1)S(1)}, f32[3,64,512]{2,1,0:T(8,128)S(1)}) custom-call(s32[64]{0:T(128)} %block_any.1, s32[1,64]{1,0:T(1,128)} %bitcast.10, f32[1,512]{1,0:T(1,128)} %bitcast.9, s32[64,512]{1,0:T(8,128)} %cell_any.1, f32[64,512]{1,0:T(8,128)} %place_any.1, f32[64,512]{1,0:T(8,128)} %volume_any.1, f32[64,512]{1,0:T(8,128)} %rate_any.1, ...), custom_call_target="tpu_custom_call" | custom-call | tf_op jit(solution)/shard_map/flow/pallas_call | solution.py:573
  42.8 1.3 %deliver.1 = (bf16[8,3,256,128]{3,2,1,0:T(8,128)(2,1)}, f32[3,64,512]{2,1,0:T(8,128)}) custom-call(bf16[8,3,256,128]{3,2,1,0:T(8,128)(2,1)S(1)} %get-tuple-element.6.planes, f32[3,64,512]{2,1,0:T(8,128)S(1)} %get-tuple-element.7.updated), custom_call_target="tpu_custom_call" | custom-call | tf_op jit(solution)/shard_map/deliver/pallas_call | solution.py:614

commit v6 on v5

--- a/solution.py
+++ b/solution.py
@@ -126,6 +126,7 @@
     block_any,
     block_line_any,
     eigenvalues_any,
+    tables_back_any,
     cell_any,
     place_any,
     volume_any,
@@ -142,6 +143,7 @@
     block,
     block_line,
     eigenvalues,
+    tables_back,
     cell,
     place,
     volume,
@@ -185,9 +187,9 @@
         return lax.rem(px + step // N_PZ, N_PX), lax.rem(pz + lax.rem(step, N_PZ), N_PZ)
 
     sources = (cell_any, place_any, volume_any, rate_any, motion_any, seen_any)
-    sources += (block_line_any, block_any, eigenvalues_any, tables_any, order_any, fluid_any, basis_any, inverse_any)
+    sources += (block_line_any, block_any, eigenvalues_any, tables_back_any, tables_any, order_any, fluid_any, basis_any, inverse_any)
     targets = (cell, place, volume, rate, motion, seen)
-    targets += (block_line, block, eigenvalues, tables, order, fluid, basis, inverse)
+    targets += (block_line, block, eigenvalues, tables_back, tables, order, fluid, basis, inverse)
     loads = [
         pltpu.make_async_copy(source, target, load_sem.at[i])
         for i, (source, target) in enumerate(zip(sources, targets))
@@ -402,8 +404,8 @@
         re, im = [], []
         for q in range(4):
             rows = jnp.concatenate([halves[0][q], halves[1][q]], axis=1)
-            even = dot_t(rows, tables[q, 0]).reshape(MODES, 2, ROWS, FOLD)
-            odd = dot_t(rows, tables[q, 1]).reshape(MODES, 2, ROWS, FOLD)
+            even = dot(rows, tables_back[q, 0]).reshape(MODES, 2, ROWS, FOLD)
+            odd = dot(rows, tables_back[q, 1]).reshape(MODES, 2, ROWS, FOLD)
             re.append(even[:, 0] - odd[:, 1])
             im.append(odd[:, 0] + even[:, 1])
         sums = (re[0] + re[2], im[0] + im[2])
@@ -421,24 +423,26 @@
                 for m in range(MODES):
                     for t in range(4):
                         planes[
-                            pl.ds(m * 32 + (4 * j + t) * 2 + r, ROWS, stride=MODES * 32), :
+                            pl.ds(m * 33 + (4 * j + t) * 2 + r, ROWS, stride=265), :
                         ] = results[j][r][m, :, 128 * t : 128 * t + 128]
 
-        def one_row(y, carry):
-            first = pl.multiple_of(y * MODES * 32, MODES * 32)
-            planes_out[y, c] = planes[pl.ds(first, MODES * 32), :].astype(bf16)
+        for y in range(ROWS):
             for s in range(STRIPS):
                 for h in range(2):
                     pair = [
-                        planes[pl.ds(first + (2 * s + h) * 2 + r, MODES, stride=32), :]
+                        planes[pl.ds(y * 265 + (2 * s + h) * 2 + r, MODES, stride=33), :]
                         for r in range(2)
                     ]
                     blocks[c, y * STRIPS + s, :, 128 * h : 128 * h + 128] = jnp.concatenate(
                         pair, axis=0
                     ).astype(bf16)
-            return carry
-
-        lax.fori_loop(0, ROWS, one_row, 0)
+
+    def write_planes(c):
+        for y in range(ROWS):
+            for m in range(MODES):
+                planes_out[y, c, m * 32 : m * 32 + 32] = planes[
+                    pl.ds(y * 265 + m * 33, 32), :
+                ].astype(bf16)
 
     def part_copy(group, turn):
         here = (pl.ds(group[0], len(group)), pl.ds(pl.multiple_of(turn * 16, 16), 16))
@@ -501,7 +505,10 @@
         for c in group:
             exchange_wait(3 + c)
             backward(c)
+            if c < 2:
+                write_planes(c)
         sample(group)
+    write_planes(2)
     for group in PASSES:
         update(group)
     for index in range(6):
@@ -536,12 +543,14 @@
     eigenvalues,
 ):
     tables = jnp.asarray(wave_tables())
+    tables_back = jnp.asarray(np.swapaxes(wave_tables(), 2, 3).copy())
     order = jnp.asarray(lane_order())
     particles = ((TILES, PT), f32)
     vectors = ((3, TILES, PT), f32)
     scratch = (
         ((1, TILES), jnp.int32),
         ((1, NY), f32),
+        (tables_back.shape, bf16),
         ((TILES, PT), jnp.int32),
         particles,
         particles,
@@ -564,7 +573,7 @@
         ((3, SLABS, 16, 128), bf16),
         ((3, SLABS, 16, 128), bf16),
         ((3, MODES, 16, KX), bf16),
-        ((ROWS * MODES * 32, 128), f32),
+        ((2120, 128), f32),
         ((3, BLOCKS, 16, CB), bf16),
         vectors,
         ((3, TILES, PT), bf16),
@@ -576,12 +585,12 @@
             jax.ShapeDtypeStruct((ROWS, 3, MODES * 32, 128), bf16),
             jax.ShapeDtypeStruct((3, TILES, PT), f32),
         ),
-        in_specs=[HBM] * 14,
+        in_specs=[HBM] * 15,
         out_specs=(VMEM, VMEM),
         scratch_shapes=[pltpu.SMEM((TILES,), jnp.int32)]
         + [pltpu.VMEM(*item) for item in scratch]
         + [
-            pltpu.SemaphoreType.DMA((14,)),
+            pltpu.SemaphoreType.DMA((15,)),
             pltpu.SemaphoreType.DMA((6,)),
             pltpu.SemaphoreType.DMA((6,)),
             pltpu.SemaphoreType.DMA((6,)),
@@ -598,6 +607,7 @@
         block_index,
         block_index.reshape(1, TILES),
         eigenvalues.reshape(1, NY),
+        tables_back,
         cell_index,
         spanwise_position,
         volume,

time: 44.2 us -> 41.7 us (0.943)
  Pallas kernels: 43.4 us -> 40.9 us
    pallas_call x1, Pallas kernels: 42.1 us -> 39.6 us  [on_device(): pl.pallas_call(flow_kernel, out_shape=(jax.ShapeDtypeStruct((ROWS, 3, MOD...]
where the time goes in v6:
time: 41.7 us; the launch traced here: 41.6 us
  Pallas kernels  40.9 us (98%)
  between operations  0.64 us (2%)
    pallas_call x1, Pallas kernels, on_device(): pl.pallas_call(flow_kernel, out_shape=(jax.ShapeDtypeStruct((ROWS, 3, MOD...  39.6 us
    pallas_call x1, Pallas kernels, on_device(): pl.pallas_call(deliver_kernel, out_shape=(jax.ShapeDtypeStruct(planes.sha...  1.31 us

profile of v6, /device:TPU:1, one launch (start us, length us, event | category | flops | bytes accessed | tf_op | source)
XLA Modules:
  0.0 41.6 jit_solution(7710249561268980181)
XLA Ops:
  0.6 39.6 %flow.1 = (bf16[8,3,256,128]{3,2,1,0:T(8,128)(2,1)S(1)}, f32[3,64,512]{2,1,0:T(8,128)S(1)}) custom-call(s32[64]{0:T(128)} %block_any.1, s32[1,64]{1,0:T(1,128)} %bitcast.9, f32[1,512]{1,0:T(1,128)} %bitcast.10, bf16[4,2,256,512]{3,2,1,0:T(8,128)(2,1)} %constant.7.clone.tables_back_any, s32[64,512]{1,0:T(8,128)} %cell_any.1, f32[64,512]{1,0:T(8,128)} %place_any.1, ...), custom_call_target="tpu_custom_call" | custom-call | tf_op jit(solution)/shard_map/flow/pallas_call | solution.py:582
  40.2 1.3 %deliver.1 = (bf16[8,3,256,128]{3,2,1,0:T(8,128)(2,1)}, f32[3,64,512]{2,1,0:T(8,128)}) custom-call(bf16[8,3,256,128]{3,2,1,0:T(8,128)(2,1)S(1)} %get-tuple-element.6.planes, f32[3,64,512]{2,1,0:T(8,128)S(1)} %get-tuple-element.7.updated), custom_call_target="tpu_custom_call" | custom-call | tf_op jit(solution)/shard_map/deliver/pallas_call | solution.py:624

commit v7 on v6

--- a/solution.py
+++ b/solution.py
@@ -194,7 +194,7 @@
         pltpu.make_async_copy(source, target, load_sem.at[i])
         for i, (source, target) in enumerate(zip(sources, targets))
     ]
-    for load in loads:
+    for load in loads[:7]:
         load.start()
 
     barrier = pltpu.get_barrier_semaphore()
@@ -210,6 +210,8 @@
     wave, shift = mode_turns(grp)
     for load in loads[:7]:
         load.wait()
+    for load in loads[7:]:
+        load.start()
     selection = block_fold(block_line[...])
 
     def deposit(turn, carry):

time: 41.7 us -> 41.7 us (level)
  no operation moved by 1% of the time
where the time goes in v7:
time: 41.7 us; the launch traced here: 41.6 us
  Pallas kernels  40.9 us (98%)
  between operations  0.64 us (2%)
    pallas_call x1, Pallas kernels, on_device(): pl.pallas_call(flow_kernel, out_shape=(jax.ShapeDtypeStruct((ROWS, 3, MOD...  39.6 us
    pallas_call x1, Pallas kernels, on_device(): pl.pallas_call(deliver_kernel, out_shape=(jax.ShapeDtypeStruct(planes.sha...  1.31 us

profile of v7, /device:TPU:1, one launch (start us, length us, event | category | flops | bytes accessed | tf_op | source)
XLA Modules:
  0.0 41.6 jit_solution(6694788816321965955)
XLA Ops:
  0.6 39.6 %flow.1 = (bf16[8,3,256,128]{3,2,1,0:T(8,128)(2,1)S(1)}, f32[3,64,512]{2,1,0:T(8,128)S(1)}) custom-call(s32[64]{0:T(128)} %block_any.1, s32[1,64]{1,0:T(1,128)} %bitcast.9, f32[1,512]{1,0:T(1,128)} %bitcast.10, bf16[4,2,256,512]{3,2,1,0:T(8,128)(2,1)} %constant.7.clone.tables_back_any, s32[64,512]{1,0:T(8,128)} %cell_any.1, f32[64,512]{1,0:T(8,128)} %place_any.1, ...), custom_call_target="tpu_custom_call" | custom-call | tf_op jit(solution)/shard_map/flow/pallas_call | solution.py:584
  40.2 1.3 %deliver.1 = (bf16[8,3,256,128]{3,2,1,0:T(8,128)(2,1)}, f32[3,64,512]{2,1,0:T(8,128)}) custom-call(bf16[8,3,256,128]{3,2,1,0:T(8,128)(2,1)S(1)} %get-tuple-element.6.planes, f32[3,64,512]{2,1,0:T(8,128)S(1)} %get-tuple-element.7.updated), custom_call_target="tpu_custom_call" | custom-call | tf_op jit(solution)/shard_map/deliver/pallas_call | solution.py:626
